TPU v7x, 256 devices: a whole 4x4x8 slice. The times are simulated.
256 devices in a mesh: seq: 64 (over y, x_lo, z), lvl: 4 (over x_hi, core).
Axes of the slice: x: 4 (x_hi: 2, x_lo: 2; x = x_hi * 2 + x_lo), y: 4, z: 8, core: 2. Of those that a mesh axis runs over, the one named last changes fastest.
Arguments:
- hidden: bfloat16 [8192, 4096], P('seq', 'lvl'), may hold values from -6 to 6
- code_ids: int32 [8192, 4], P('seq'), may hold values from 0 to 2047
- lengths: int32 [4], replicated, may hold values from 1 to 4096, 8192 in all
- weight_in: bfloat16 [4096, 1024], P('lvl'), may hold values from -0.09375 to 0.09375
- weight_query: bfloat16 [1024, 1024], P(None, 'lvl'), may hold values from -0.1875 to 0.1875
- weight_key: bfloat16 [1024, 1024], P(None, 'lvl'), may hold values from -0.1875 to 0.1875
- weight_value: bfloat16 [1024, 1024], P(None, 'lvl'), may hold values from -0.1875 to 0.1875
- weight_out: bfloat16 [1024, 1024], P('lvl'), may hold values from -0.1875 to 0.1875
- norm_gain: float32 [1024], replicated, may hold values from 0.1 to 1.9
- tables: bfloat16 [2048, 4, 1024], P('seq', None, 'lvl'), may hold values from -6 to 6
- upstream: bfloat16 [8192, 4, 1024], P(('seq', 'lvl')), may hold values from -6 to 6
Outputs:
- output: bfloat16 [8192, 4, 1024], P(('seq', 'lvl'))
- hidden_grad: bfloat16 [8192, 4096], P('seq', 'lvl')
- table_grad: float32 [2048, 4, 1024], P('seq', None, 'lvl')
Inputs may be any that keep to these rules, and one draw needn't show every extreme that they name: Dialogue lengths in frames; they sum to 8192 and the longest has exactly 4096 frames.
All inputs are finite; a program needn't handle non-finite values.
Results may differ from a plain program's by a relative error of at most 0.02.
Values may be sent and summed in bfloat16 or wider, within the bound.
A program may use at most 128 MiB of HBM per device.

v0:
```python
import math

import jax
import jax.numpy as jnp
from jax import lax
from jax.sharding import PartitionSpec as P

HEADS = 16


EPSILON = 1e-05


def passed_along(block, axis, distance):
    devices = range(lax.axis_size(axis))
    route = [(i - distance, i) for i in devices if i - distance in devices]
    return lax.ppermute(block, axis, route)


def to_heads(tensor, head_size):
    return tensor.reshape(tensor.shape[0], tensor.shape[1], tensor.shape[2] // head_size, head_size)


def attend(normed, weight_query, weight_key, weight_value, head_size):
    frames, levels = (normed.shape[0], normed.shape[1])
    scaling = 1.0 / math.sqrt(head_size)
    query_rows = jnp.einsum(
        "flc,cd->fld", normed, weight_query, preferred_element_type=jnp.float32
    ).astype(jnp.bfloat16)
    key_rows = jnp.einsum(
        "flc,cd->fld", normed, weight_key, preferred_element_type=jnp.float32
    ).astype(jnp.bfloat16)
    value_rows = jnp.einsum(
        "flc,cd->fld", normed, weight_value, preferred_element_type=jnp.float32
    ).astype(jnp.bfloat16)
    scores = (
        jnp.einsum(
            "flhs,fmhs->fhlm",
            to_heads(query_rows, head_size),
            to_heads(key_rows, head_size),
            preferred_element_type=jnp.float32,
        )
        * scaling
    )
    causal = jnp.arange(levels)[None, :] <= jnp.arange(levels)[:, None]
    raised = jnp.where(causal, jnp.exp(scores), 0.0)
    weights = raised / jnp.sum(raised, axis=-1, keepdims=True)
    weights_bf = weights.astype(jnp.bfloat16)
    mixture = jnp.einsum(
        "fhlm,fmhs->flhs",
        weights_bf,
        to_heads(value_rows, head_size),
        preferred_element_type=jnp.float32,
    )
    mixture = mixture.astype(jnp.bfloat16).reshape(frames, levels, query_rows.shape[2])
    return (query_rows, key_rows, value_rows, weights, weights_bf, mixture)


def attend_back(grad_mixture, saved, weight_query, weight_key, weight_value, head_size):
    query_rows, key_rows, value_rows, weights, weights_bf, mixture = saved
    scaling = 1.0 / math.sqrt(head_size)
    grad_heads = to_heads(grad_mixture, head_size)
    grad_weights = jnp.einsum(
        "flhs,fmhs->fhlm",
        grad_heads,
        to_heads(value_rows, head_size),
        preferred_element_type=jnp.float32,
    )
    grad_value = jnp.einsum(
        "fhlm,flhs->fmhs", weights_bf, grad_heads, preferred_element_type=jnp.float32
    ).astype(jnp.bfloat16)
    grad_scores = (
        weights * (grad_weights - jnp.sum(weights * grad_weights, axis=-1, keepdims=True)) * scaling
    ).astype(jnp.bfloat16)
    grad_query = jnp.einsum(
        "fhlm,fmhs->flhs",
        grad_scores,
        to_heads(key_rows, head_size),
        preferred_element_type=jnp.float32,
    ).astype(jnp.bfloat16)
    grad_key = jnp.einsum(
        "fhlm,flhs->fmhs",
        grad_scores,
        to_heads(query_rows, head_size),
        preferred_element_type=jnp.float32,
    ).astype(jnp.bfloat16)
    flat_shape = grad_mixture.shape
    partial_normed = jnp.einsum(
        "fld,cd->flc",
        grad_query.reshape(flat_shape),
        weight_query,
        preferred_element_type=jnp.float32,
    )
    partial_normed = partial_normed + jnp.einsum(
        "fld,cd->flc", grad_key.reshape(flat_shape), weight_key, preferred_element_type=jnp.float32
    )
    partial_normed = partial_normed + jnp.einsum(
        "fld,cd->flc",
        grad_value.reshape(flat_shape),
        weight_value,
        preferred_element_type=jnp.float32,
    )
    return partial_normed


def shards(
    hidden,
    code_ids,
    lengths,
    weight_in,
    weight_query,
    weight_key,
    weight_value,
    weight_out,
    norm_gain,
    tables,
    upstream,
):
    frames, levels = code_ids.shape
    model_width = weight_in.shape[1]
    column_count = tables.shape[2]
    vocab_rows = tables.shape[0]
    groups = lax.axis_size("lvl")
    member = lax.axis_index("lvl")
    seq_index = lax.axis_index("seq")
    head_size = model_width // HEADS
    share = frames // groups
    last_codes = passed_along(code_ids[frames - 1 :, :], "seq", 1)
    earlier = jnp.concatenate([last_codes[:, levels - 1], code_ids[: frames - 1, levels - 1]])
    previous = jnp.concatenate([earlier[:, None], code_ids[:, : levels - 1]], axis=1)
    starts = jnp.cumsum(lengths) - lengths
    position = seq_index * frames + jnp.arange(frames, dtype=jnp.int32)
    begins = jnp.any(position[:, None] == starts[None, :], axis=1)
    first_level = jnp.where(begins, 0.0, 1.0).astype(jnp.float32)
    retain = jnp.concatenate(
        [first_level[:, None], jnp.ones((frames, levels - 1), jnp.float32)], axis=1
    )[:, :, None]
    portion = lax.all_gather(tables, "seq", axis=0, tiled=True)
    choose = (previous[:, :, None] == jnp.arange(portion.shape[0], dtype=jnp.int32)).astype(
        jnp.bfloat16
    )
    looked = jnp.einsum("flr,rlc->flc", choose, portion, preferred_element_type=jnp.float32)
    context = lax.psum(
        jnp.dot(hidden, weight_in, preferred_element_type=jnp.float32).astype(jnp.bfloat16), "lvl"
    ).astype(jnp.float32)
    embedded = lax.all_gather(looked.astype(jnp.bfloat16), "lvl", axis=2, tiled=True)
    stream = context[:, None, :] + retain * embedded.astype(jnp.float32)
    scaler = lax.rsqrt(jnp.mean(stream * stream, axis=-1, keepdims=True) + EPSILON)
    unit_rows = stream * scaler
    normed = (unit_rows * norm_gain).astype(jnp.bfloat16)
    saved = attend(normed, weight_query, weight_key, weight_value, head_size)
    mixture = saved[5]
    summed = lax.psum_scatter(
        jnp.einsum("flc,cd->fld", mixture, weight_out, preferred_element_type=jnp.float32).astype(
            jnp.bfloat16
        ),
        "lvl",
        scatter_dimension=0,
        tiled=True,
    ).astype(jnp.float32)
    own_rows = lax.dynamic_slice_in_dim(stream, member * share, share, 0)
    output = (own_rows + summed).astype(jnp.bfloat16)
    upstream_all = lax.all_gather(upstream, "lvl", axis=0, tiled=True)
    grad_mixture = jnp.einsum(
        "fld,cd->flc", upstream_all, weight_out, preferred_element_type=jnp.float32
    ).astype(jnp.bfloat16)
    partial_normed = attend_back(
        grad_mixture, saved, weight_query, weight_key, weight_value, head_size
    )
    column_start = member * column_count
    grad_normed = lax.psum(partial_normed.astype(jnp.bfloat16), "lvl").astype(jnp.float32)
    grad_unit = norm_gain * grad_normed
    row_stat = jnp.mean(unit_rows * grad_unit, axis=-1, keepdims=True)
    grad_stream = upstream_all.astype(jnp.float32) + scaler * (grad_unit - unit_rows * row_stat)
    embed_grad = (
        retain * lax.dynamic_slice_in_dim(grad_stream, column_start, column_count, 2)
    ).astype(jnp.bfloat16)
    context_grad = jnp.sum(grad_stream, axis=1).astype(jnp.bfloat16)
    hidden_grad = jnp.einsum(
        "fc,dc->fd", context_grad, weight_in, preferred_element_type=jnp.float32
    ).astype(jnp.bfloat16)
    choose = (
        previous[:, :, None] == jnp.arange(vocab_rows * lax.axis_size("seq"), dtype=jnp.int32)
    ).astype(jnp.bfloat16)
    table_grad = lax.psum_scatter(
        jnp.einsum("flr,flc->rlc", choose, embed_grad, preferred_element_type=jnp.float32),
        "seq",
        scatter_dimension=0,
        tiled=True,
    )
    return (output, hidden_grad, table_grad)


def solution(mesh):
    placed = (
        P("seq", "lvl"),
        P("seq", None),
        P(),
        P("lvl", None),
        P(None, "lvl"),
        P(None, "lvl"),
        P(None, "lvl"),
        P("lvl", None),
        P(),
        P("seq", None, "lvl"),
        P(("seq", "lvl"), None, None),
    )
    return jax.shard_map(
        shards,
        mesh=mesh,
        in_specs=placed,
        out_specs=(P(("seq", "lvl"), None, None), P("seq", "lvl"), P("seq", None, "lvl")),
        check_vma=False,
    )
```

profile of v0, /device:TPU:4, one launch (start us, length us, event | category | flops | bytes accessed | tf_op | source)
XLA Modules:
  0.0 1125.8 jit_solution(6483171158836035957)
XLA Ops:
  8.1 1.6 copy.83
  9.8 2.1 convolution_convert_fusion.10
  12.9 3.8 collective-permute-start
  19.3 298.8 %all-gather.4.cloned.1.call-done = bf16[2048,4,256]{2,0,1:T(8,128)(2,1)} async-done(((bf16[32,4,256]{2,0,1:T(8,128)(2,1)}), bf16[2048,4,256]{2,0,1:T(8,128)(2,1)}) %all-gather.4.cloned.1.call-update) | async-done | bytes 4194320 | tf_op jit(solution)/shard_map/all_gather | solution.py:138
  318.1 3.7 fusion.15
  323.3 14.6 %all-gather.8.cloned.1.call-done = bf16[128,4,1024]{2,0,1:T(8,128)(2,1)} async-done(((bf16[32,4,1024]{2,0,1:T(8,128)(2,1)}), bf16[128,4,1024]{2,0,1:T(8,128)(2,1)}) %all-gather.8.cloned.1.call-update) | async-done | bytes 1048592 | tf_op jit(solution)/shard_map/all_gather | solution.py:163
  337.9 1.7 convolution_convert_fusion.6
  341.0 22.4 %all-gather.6.cloned.1.call-done = bf16[128,4,1024]{2,0,1:T(8,128)(2,1)} async-done(((bf16[128,4,256]{2,0,1:T(8,128)(2,1)}), bf16[128,4,1024]{2,0,1:T(8,128)(2,1)}) %all-gather.6.cloned.1.call-update) | async-done | bytes 1048592 | tf_op jit(solution)/shard_map/all_gather | solution.py:146
  363.3 1.7 multiply_reduce_fusion.1
  365.1 2.9 convolution_convert_fusion.9
  370.3 2.5 convolution_convert_fusion.8
  375.2 2.5 convolution_convert_fusion.7
  380.0 2.9 fusion.45
  382.9 3.7 fusion.32
  386.6 4.5 fusion.11
  391.1 4.4 fusion.12
  395.5 2.9 fusion.13
  398.4 1.5 copy.99
  399.9 2.9 fusion.26
  404.2 2.8 fusion.23
  408.5 4.1 add_convert_fusion
  412.6 3.0 fusion.10
  417.1 2.5 convolution_convert_fusion
  419.7 43.8 %all-reduce.8.cloned.1.call-done = bf16[128,4,1024]{2,0,1:T(8,128)(2,1)} async-done(((bf16[128,4,1024]{2,0,1:T(8,128)(2,1)}), bf16[128,4,1024]{2,0,1:T(8,128)(2,1)}) %all-reduce.8.cloned.1.call-update) | async-done | bytes 1048592 | tf_op jit(solution)/shard_map/psum | solution.py:171
  463.5 2.2 multiply_reduce_fusion
  465.7 2.3 fusion.44
  468.0 4.6 convolution_bitcast_fusion
  472.6 10.0 copy.108
  484.5 1.5 convolution_convert_fusion.5
  486.1 17.8 %reduce-scatter.2.cloned.1.call-done = bf16[32,4,1024]{2,0,1:T(8,128)(2,1)} async-done(((bf16[128,4,1024]{2,0,1:T(8,128)(2,1)}), bf16[32,4,1024]{2,0,1:T(8,128)(2,1)}) %reduce-scatter.2.cloned.1.call-update) | async-done | bytes 262160 | tf_op jit(solution)/shard_map/reduce_scatter | solution.py:153
  506.0 610.9 %all-reduce.10.cloned.1.call-done = f32[2048,4,256]{2,1,0:T(4,128)} async-done(((f32[2048,4,256]{2,1,0:T(4,128)}), f32[2048,4,256]{2,1,0:T(4,128)}) %all-reduce.10.cloned.1.call-update) | async-done | bytes 8388624
  1116.9 1.6 constant_dynamic-slice_fusion
  (70 shorter events, 21.3 us)
Async XLA Ops:
  8.0 1.8 copy-start
  8.0 4.0 copy-start.7
  8.0 4.8 copy-start.9
  8.0 310.1 %all-gather.4.cloned.1.call-start = ((), (), s32[]{:S(2)}) async-start(), calls=%async_computation.2 | async-start | bytes 4259840 | tf_op jit(solution)/shard_map/all_gather | solution.py:138
  9.7 312.5 %all-reduce.6.cloned.1.call-start = ((), (), s32[]{:S(2)}) async-start(), calls=%async_computation.1 | async-start | bytes 524288 | tf_op jit(solution)/shard_map/psum | solution.py:143
  11.9 325.9 %all-gather.8.cloned.1.call-start = ((), (), s32[]{:S(2)}) async-start(), calls=%async_computation.5 | async-start | bytes 1310720 | tf_op jit(solution)/shard_map/all_gather | solution.py:163
  12.8 350.5 %all-gather.6.cloned.1.call-start = ((), (), s32[]{:S(2)}) async-start(), calls=%async_computation.3 | async-start | bytes 1310720 | tf_op jit(solution)/shard_map/all_gather | solution.py:146
  12.9 5.1 collective-permute-start
  19.3 302.6 %copy-start.10 = (s32[4]{0:T(128)S(1)}, s32[4]{0:T(128)}, u32[]{:S(2)}) copy-start(s32[4]{0:T(128)} %param.13) | copy-start | bytes 52
  19.3 318.6 %copy-start.6 = (bf16[256,1024]{1,0:T(8,128)(2,1)S(1)}, bf16[256,1024]{1,0:T(8,128)(2,1)}, u32[]{:S(2)}) copy-start(bf16[256,1024]{1,0:T(8,128)(2,1)} %param.18) | copy-start | bytes 1572868
  321.8 141.7 %all-reduce.8.cloned.1.call-start = ((), (), s32[]{:S(2)}) async-start(), calls=%async_computation.6 | async-start | bytes 2097152 | tf_op jit(solution)/shard_map/psum | solution.py:171
  323.2 41.8 %copy-start.2 = (f32[128,1024]{1,0:T(8,128)}, f32[128,1024]{1,0:T(8,128)S(1)}, u32[]{:S(2)}) copy-start(f32[128,1024]{1,0:T(8,128)S(1)} %convert_element_type.90) | copy-start | bytes 1572868
  323.3 41.8 %copy-start.8 = (f32[1024]{0:T(1024)S(1)}, f32[1024]{0:T(1024)}, u32[]{:S(2)}) copy-start(f32[1024]{0:T(1024)} %param.19) | copy-start | bytes 12292
  365.1 5.2 copy-start.1
  412.6 91.3 %reduce-scatter.2.cloned.1.call-start = ((), (), s32[]{:S(2)}) async-start(), calls=%async_computation.4 | async-start | bytes 1310720 | tf_op jit(solution)/shard_map/reduce_scatter | solution.py:153
  419.6 697.3 %all-reduce.10.cloned.1.call-start = ((), (), s32[]{:S(2)}) async-start(), calls=%async_computation.7 | async-start | bytes 16777216
  463.5 2.2 copy-start.3
  463.5 2.2 copy-start.4
  463.5 2.2 copy-start.5
  482.6 0.7 copy-start.11
Sparse Core Ops, SparseCore 0:
  11.4 306.7 all-gather.3
  320.1 17.7 all-gather.7
  340.4 22.8 all-gather.5
  482.8 634.0 all-reduce.9
Sparse Core Ops, SparseCore 1:
  13.4 46.1 all-reduce.5
  412.7 50.8 all-reduce.7
  466.1 37.7 reduce-scatter.1
where the time goes:
time: 1130 us
  waiting for transfers between devices  1010 us (89%)
  matrix products  55.2 us (5%)
  local copies, waits for them, and re-layouts  31 us (3%)
  between operations  16.4 us (1%)
    unnamed x8, waiting for transfers between devices  611 us
    all_gather x1, waiting for transfers between devices, shards(): portion = lax.all_gather(tables, 'seq', axis=0, tiled=True)  299 us
    psum x1, waiting for transfers between devices, shards(): lax.psum(partial_normed.astype(jnp.bfloat16), 'lvl').astype(jnp.float32)  43.8 us
  transfers between devices with their start and end apart: 8, of which 7 were waited for; matrix products, arithmetic and copies ran while one was open for 4% of the time, Pallas kernels for 0%

commit v1 on v0

v1 whole, which is shorter than its diff:
```python
import math

import jax
import jax.numpy as jnp
from jax import lax
from jax.experimental import pallas as pl
from jax.experimental.pallas import tpu as pltpu
from jax.sharding import PartitionSpec as P

HEADS = 16
EPSILON = 1e-05
MESH = pl.DeviceIdType.MESH
F32 = jnp.float32
BF16 = jnp.bfloat16

NY, NZ = 4, 8
LV = 4
FR = 128
OWN = 32
COLS = 256
WIDTH = 1024
ENT = 32
RANGE = 512
PAIRS = [(a, b) for a in range(LV) for b in range(a + 1)]


def dot(a, b):
    return lax.dot_general(a, b, (((1,), (0,)), ((), ())), preferred_element_type=F32)


def dot_nt(a, b):
    return lax.dot_general(a, b, (((1,), (1,)), ((), ())), preferred_element_type=F32)


def kernel(
    codes_ref, lens_ref, gain_ref, tab_ref, up_ref, hid_ref, win_hbm, wq_hbm, wk_hbm, wv_hbm, wo_hbm,
    out_ref, hg_ref, tg_ref,
    win, wq, wk, wv, wo,
    nbr, prev, tab, oh, oht, ups, ctx_send, ctx_recv,
    look, relay, fin, stream_own, streams, normed, scale,
    qs, ks, vs, gms, prod, sums, mix, gqs, gks, gvs,
    pn, pn_own, pn_core, pn_mid, pn_x, stat_wide, stat, stat_col,
    opart, o_core, o_mid, o_x,
    eg, cgs, grads, zs_send, zs_recv, xs_send, xs_recv,
    local_sem, ssem, rsem,
):
    seq = lax.axis_index("seq")
    lvl = lax.axis_index("lvl")
    y = lax.div(seq, 16)
    xl = lax.rem(lax.div(seq, 8), 2)
    z = lax.rem(seq, 8)
    xh = lax.div(lvl, 2)
    core = lax.rem(lvl, 2)

    def device(dy=0, dx=0, dz=0, dh=0, dc=0):
        yy = lax.rem(y + dy + NY, NY)
        xx = 1 - xl if dx else xl
        zz = lax.rem(z + dz + NZ, NZ)
        hh = 1 - xh if dh else xh
        cc = 1 - core if dc else core
        return (yy * 16 + xx * 8 + zz, hh * 2 + cc)

    seq_next = (lax.rem(seq + 1, 64), lvl)
    seq_back = (lax.rem(seq + 63, 64), lvl)
    y_up, y_down, y_far = device(dy=1), device(dy=-1), device(dy=2)
    z_up, z_down = device(dz=1), device(dz=-1)
    x_near, x_far, mate, cross = device(dx=1), device(dh=1), device(dc=1), device(dh=1, dc=1)
    lvl_far = (1 - xh) * 2 + core
    lvl_mate = xh * 2 + 1 - core
    lvl_cross = (1 - xh) * 2 + 1 - core

    started = []

    def send(src, dst, target):
        i = len(started)
        copy = pltpu.make_async_remote_copy(
            src_ref=src, dst_ref=dst, send_sem=ssem.at[i], recv_sem=rsem.at[i],
            device_id=target, device_id_type=MESH,
        )
        copy.start()
        started.append(copy)
        return copy

    fetch = [
        pltpu.make_async_copy(a, b, local_sem.at[i])
        for i, (a, b) in enumerate(
            ((win_hbm, win), (wo_hbm, wo), (wq_hbm, wq), (wk_hbm, wk), (wv_hbm, wv))
        )
    ]
    for copy in fetch:
        copy.start()

    barrier = pltpu.get_barrier_semaphore()
    for source in (z_up, z_down, x_near, y_up, y_down, y_far, mate, x_far, cross, seq_back):
        pl.semaphore_signal(barrier, inc=1, device_id=source, device_id_type=MESH)

    def rows(start, size):
        return pl.ds(pl.multiple_of(start, size), size)

    def block_rows(xx, zz):
        return rows((xx * 8 + lax.rem(zz + NZ, NZ)) * ENT, ENT)

    own_rows = block_rows(xl, z)
    own_frames = rows(lvl * OWN, OWN)
    tab[:, own_rows, :] = tab_ref[...]
    ups[:, own_frames, :] = up_ref[...]

    pl.semaphore_wait(barrier, 10)

    code_copy = send(codes_ref, nbr, seq_next)
    x_copy = send(tab.at[:, own_rows], tab.at[:, own_rows], x_near)
    plus, minus = [], []
    plus.append([send(tab.at[:, own_rows], tab.at[:, own_rows], z_up)])
    minus.append([send(tab.at[:, own_rows], tab.at[:, own_rows], z_down)])
    up_far = send(ups.at[:, own_frames], ups.at[:, own_frames], x_far)
    up_mate = send(ups.at[:, own_frames], ups.at[:, own_frames], mate)

    fetch[0].wait()
    part = dot(hid_ref[...], win[...])
    for b in range(4):
        ctx_send[b] = part[:, b * COLS : (b + 1) * COLS].astype(BF16)
    ctx_copies = [
        send(ctx_send.at[lvl_far], ctx_recv.at[0], x_far),
        send(ctx_send.at[lvl_mate], ctx_recv.at[1], mate),
        send(ctx_send.at[lvl_cross], ctx_recv.at[2], cross),
    ]

    x_copy.wait_recv()
    near_rows = block_rows(1 - xl, z)
    plus[0].append(send(tab.at[:, near_rows], tab.at[:, near_rows], z_up))
    minus[0].append(send(tab.at[:, near_rows], tab.at[:, near_rows], z_down))

    code_copy.wait_recv()
    lane8 = lax.broadcasted_iota(jnp.int32, (8, FR), 1)
    sub8 = lax.broadcasted_iota(jnp.int32, (8, FR), 0)
    own_codes = codes_ref[...]
    shifted = pltpu.roll(own_codes, 1, 1)
    incoming = pltpu.roll(nbr[...], 1, 1)
    incoming = jnp.where(jnp.broadcast_to(seq, (8, FR)) == 0, 0, incoming)
    shifted = jnp.where(lane8 == 0, incoming, shifted)
    first_row = jnp.broadcast_to(shifted[LV - 1 : LV, :], (8, FR))
    prev[0] = jnp.where(sub8 == 0, first_row, pltpu.roll(own_codes, 1, 0))
    code_y = [
        send(prev.at[0], prev.at[1], y_up),
        send(prev.at[0], prev.at[2], y_down),
        send(prev.at[0], prev.at[3], y_far),
    ]

    def ring(t):
        last_plus, last_minus = plus[t - 1], minus[t - 1]
        new_plus, new_minus = [], []
        for j, xx in enumerate((xl, 1 - xl)):
            last_plus[j].wait_recv()
            block = block_rows(xx, z - t)
            new_plus.append(send(tab.at[:, block], tab.at[:, block], z_up))
            last_minus[j].wait_recv()
            if t < 3:
                block = block_rows(xx, z + t)
                new_minus.append(send(tab.at[:, block], tab.at[:, block], z_down))
        plus.append(new_plus)
        minus.append(new_minus)

    ring(1)
    up_far.wait_recv()
    far_frames = rows(lvl_far * OWN, OWN)
    up_pass = send(ups.at[:, far_frames], ups.at[:, far_frames], mate)

    for copy in code_y:
        copy.wait_recv()
    first = y * RANGE
    by_lane = lax.broadcasted_iota(jnp.int32, (FR, RANGE), 1) + first
    by_row = lax.broadcasted_iota(jnp.int32, (RANGE, FR), 0) + first
    for slot in range(NY):
        codes = prev[slot]
        turned = jnp.transpose(
            jnp.concatenate([codes.astype(F32), jnp.zeros((FR - 8, FR), F32)], axis=0)
        ).astype(jnp.int32)
        for k in range(LV):
            column = jnp.broadcast_to(turned[:, k : k + 1], (FR, RANGE))
            oh[k, slot * FR : (slot + 1) * FR, :] = jnp.where(column == by_lane, 1.0, 0.0).astype(BF16)

    ring(2)
    for slot in range(NY):
        codes = prev[slot]
        for k in range(LV):
            row = jnp.broadcast_to(codes[k : k + 1, :], (RANGE, FR))
            oht[k, :, slot * FR : (slot + 1) * FR] = jnp.where(row == by_row, 1.0, 0.0).astype(BF16)

    ring(3)
    up_mate.wait_recv()
    up_pass.wait_recv()
    fetch[1].wait()
    for k in range(LV):
        gms[k] = dot_nt(ups[k], wo[...]).astype(BF16)
    for copy in ctx_copies:
        copy.wait_recv()
    context = (
        ctx_send[lvl].astype(F32) + ctx_recv[0].astype(F32)
        + ctx_recv[1].astype(F32) + ctx_recv[2].astype(F32)
    )
    frame = lax.broadcasted_iota(jnp.int32, (FR, COLS), 0) + seq * FR
    begin = jnp.int32(0)
    retain = jnp.ones((FR, COLS), F32)
    for i in range(4):
        retain = jnp.where(frame == begin, 0.0, retain)
        begin = begin + lens_ref[i]

    for copy in plus[3]:
        copy.wait_recv()

    step_up, step_down, last_up, last_down = [], [], [], []
    for k in range(LV):
        found = dot(oh[k], tab[k]).astype(BF16)
        for slot in range(NY):
            look[slot, k] = found[slot * FR : (slot + 1) * FR, :]
        if k < 2:
            step_up.append(send(look.at[3, k], relay.at[0, k], y_up))
            last_down.append(send(look.at[1, k], fin.at[1, k], y_down))
            last_up.append(None)
        else:
            step_down.append(send(look.at[3, k], relay.at[1, k - 2], y_down))
            last_up.append(send(look.at[2, k], fin.at[0, k], y_up))
            last_down.append(None)
    for k in range(2):
        step_up[k].wait_recv()
        look[2, k] = look[2, k] + relay[0, k]
        last_up[k] = send(look.at[2, k], fin.at[0, k], y_up)
        step_down[k].wait_recv()
        look[1, k + 2] = look[1, k + 2] + relay[1, k]
        last_down[k + 2] = send(look.at[1, k + 2], fin.at[1, k + 2], y_down)

    far, near, passed = [], [], []
    for k in range(LV):
        last_up[k].wait_recv()
        last_down[k].wait_recv()
        embedded = look[0, k].astype(F32) + fin[0, k].astype(F32) + fin[1, k].astype(F32)
        if k == 0:
            embedded = retain * embedded
        own = context + embedded
        stream_own[k] = own
        streams[lvl, k] = own.astype(BF16)
        far.append(send(streams.at[lvl, k], streams.at[lvl, k], x_far))
        near.append(send(streams.at[lvl, k], streams.at[lvl, k], mate))
    for copy in fetch[2:]:
        copy.wait()
    for k in range(LV):
        far[k].wait_recv()
        passed.append(send(streams.at[lvl_far, k], streams.at[lvl_far, k], mate))
    for k in range(LV):
        near[k].wait_recv()
        passed[k].wait_recv()

    def norm_body(i, carry):
        k = lax.div(i, 4)
        r = rows(lax.rem(i, 4) * 32, 32)
        blocks = [streams[b, k, r, :].astype(F32) for b in range(4)]
        total = blocks[0] * blocks[0]
        for b in range(1, 4):
            total = total + blocks[b] * blocks[b]
        scaler = lax.rsqrt(jnp.sum(total, axis=1, keepdims=True) * (1.0 / WIDTH) + EPSILON)
        scale[k, r, :] = jnp.broadcast_to(scaler, (32, 128))
        for b in range(4):
            normed[k, r, b * COLS : (b + 1) * COLS] = (
                blocks[b] * scaler * gain_ref[:, b * COLS : (b + 1) * COLS]
            ).astype(BF16)
        return carry

    lax.fori_loop(0, 16, norm_body, 0)

    all_normed = normed[...].reshape(LV * FR, WIDTH)
    qs[...] = dot(all_normed, wq[...]).astype(BF16).reshape(LV, FR, COLS)
    ks[...] = dot(all_normed, wk[...]).astype(BF16).reshape(LV, FR, COLS)
    vs[...] = dot(all_normed, wv[...]).astype(BF16).reshape(LV, FR, COLS)

    def product_body(i, carry):
        r = rows(i * 16, 16)
        q = [qs[k, r, :].astype(F32) for k in range(LV)]
        kk = [ks[k, r, :].astype(F32) for k in range(LV)]
        for p, (a, b) in enumerate(PAIRS):
            prod[p, r, :] = (q[a] * kk[b]).astype(BF16)
        g = [gms[k, r, :].astype(F32) for k in range(LV)]
        v = [vs[k, r, :].astype(F32) for k in range(LV)]
        for p, (a, b) in enumerate(PAIRS):
            prod[len(PAIRS) + p, r, :] = (g[a] * v[b]).astype(BF16)
        return carry

    lax.fori_loop(0, 8, product_body, 0)
    head_row = lax.shift_right_logical(lax.broadcasted_iota(jnp.int32, (COLS, COLS), 0), 6)
    head_col = lax.shift_right_logical(lax.broadcasted_iota(jnp.int32, (COLS, COLS), 1), 6)
    same_head = jnp.where(head_row == head_col, 1.0, 0.0).astype(BF16)

    def sum_body(p, carry):
        sums[p] = dot(prod[p], same_head)
        return carry

    lax.fori_loop(0, 2 * len(PAIRS), sum_body, 0)
    scaling = 1.0 / math.sqrt(WIDTH // HEADS)

    def attend_body(i, carry):
        r = rows(lax.div(i, 2) * 16, 16)
        c = rows(lax.rem(i, 2) * 128, 128)
        q = [qs[k, r, c].astype(F32) for k in range(LV)]
        kk = [ks[k, r, c].astype(F32) for k in range(LV)]
        v = [vs[k, r, c].astype(F32) for k in range(LV)]
        g = [gms[k, r, c].astype(F32) for k in range(LV)]
        grad_key = [None] * LV
        grad_value = [None] * LV
        p = 0
        for a in range(LV):
            raised = [jnp.exp(sums[p + b, r, c] * scaling) for b in range(a + 1)]
            total = raised[0]
            for b in range(1, a + 1):
                total = total + raised[b]
            inverse = 1.0 / total
            weights = [x * inverse for x in raised]
            rounded = [x.astype(BF16).astype(F32) for x in weights]
            slopes = [sums[len(PAIRS) + p + b, r, c] for b in range(a + 1)]
            mixed = rounded[0] * v[0]
            mean = weights[0] * slopes[0]
            for b in range(1, a + 1):
                mixed = mixed + rounded[b] * v[b]
                mean = mean + weights[b] * slopes[b]
            mix[a, r, c] = mixed.astype(BF16)
            grad_query = None
            for b in range(a + 1):
                grad_score = (weights[b] * (slopes[b] - mean) * scaling).astype(BF16).astype(F32)
                term_q = grad_score * kk[b]
                term_k = grad_score * q[a]
                term_v = rounded[b] * g[a]
                grad_query = term_q if b == 0 else grad_query + term_q
                grad_key[b] = term_k if a == b else grad_key[b] + term_k
                grad_value[b] = term_v if a == b else grad_value[b] + term_v
            gqs[a, r, c] = grad_query.astype(BF16)
            p += a + 1
        for b in range(LV):
            gks[b, r, c] = grad_key[b].astype(BF16)
            gvs[b, r, c] = grad_value[b].astype(BF16)
        return carry

    lax.fori_loop(0, 16, attend_body, 0)

    gq = gqs[...].reshape(LV * FR, COLS)
    gk = gks[...].reshape(LV * FR, COLS)
    gv = gvs[...].reshape(LV * FR, COLS)
    pn_copies = []
    for j, owner in enumerate((lvl_cross, lvl_mate, lvl_far, lvl)):
        w = rows(owner * COLS, COLS)
        partial = dot_nt(gq, wq[w, :]) + dot_nt(gk, wk[w, :]) + dot_nt(gv, wv[w, :])
        c = rows(owner * COLS, COLS)
        share = jnp.sum(normed[:, :, c].astype(F32).reshape(LV * FR, COLS) * partial, axis=1, keepdims=True)
        share = jnp.broadcast_to(share, (LV * FR, 128)).reshape(LV, FR, 128)
        stat_wide[...] = share if j == 0 else stat_wide[...] + share
        if j < 3:
            pn[j] = partial.astype(BF16).reshape(LV, FR, COLS)
        else:
            pn_own[...] = partial.reshape(LV, FR, COLS)
        if j < 2:
            pn_copies.append([send(pn.at[j, k], pn_core.at[j, k], mate) for k in range(LV)])
    pn_far = []
    for k in range(LV):
        pn_copies[0][k].wait_recv()
        pn_mid[k] = (pn[2, k].astype(F32) + pn_core[0, k].astype(F32)).astype(BF16)
        pn_far.append(send(pn_mid.at[k], pn_x.at[k], x_far))

    eye = lax.broadcasted_iota(jnp.int32, (FR, FR), 0) == lax.broadcasted_iota(jnp.int32, (FR, FR), 1)
    for k in range(LV):
        stat[0, k : k + 1, :] = jnp.sum(jnp.where(eye, stat_wide[k], 0.0), axis=0, keepdims=True)
    stat[0, LV:, :] = jnp.zeros((8 - LV, FR), F32)
    stat_copies = [
        send(stat.at[0], stat.at[1], x_far),
        send(stat.at[0], stat.at[2], mate),
        send(stat.at[0], stat.at[3], cross),
    ]

    opart[...] = dot(mix[...].reshape(LV * FR, COLS), wo[...]).astype(BF16).reshape(LV, FR, WIDTH)
    cross_frames = rows(lvl_cross * OWN, OWN)
    mate_frames = rows(lvl_mate * OWN, OWN)
    o_copies = [
        send(opart.at[:, cross_frames], o_core.at[0], mate),
        send(opart.at[:, mate_frames], o_core.at[1], mate),
    ]

    for copy in stat_copies:
        copy.wait_recv()
    stat_all = (stat[0] + stat[1] + stat[2] + stat[3]) * (1.0 / WIDTH)
    for k in range(LV):
        column = jnp.sum(
            jnp.where(eye, jnp.broadcast_to(stat_all[k : k + 1, :], (FR, FR)), 0.0), axis=1, keepdims=True
        )
        stat_col[k] = jnp.broadcast_to(column, (FR, 128))

    own_cols = rows(lvl * COLS, COLS)
    gain = gain_ref[:, own_cols]
    context_grad = None
    g_up, g_down = [], []
    for k in range(LV):
        pn_copies[1][k].wait_recv()
        pn_far[k].wait_recv()
        grad_normed = pn_own[k] + pn_core[1, k].astype(F32) + pn_x[k].astype(F32)
        scaler = scale[k][:, 0:1]
        unit = stream_own[k] * scaler
        grad = ups[k, :, own_cols].astype(F32) + scaler * (gain * grad_normed - unit * stat_col[k][:, 0:1])
        context_grad = grad if k == 0 else context_grad + grad
        eg[k, 0:FR, :] = (retain * grad if k == 0 else grad).astype(BF16)
        g_up.append(send(eg.at[k, 0:FR], eg.at[k, FR : 2 * FR], y_up))
        g_down.append(send(eg.at[k, 0:FR], eg.at[k, 2 * FR : 3 * FR], y_down))
    cgs[lvl] = context_grad.astype(BF16)
    cg_copies = [
        send(cgs.at[lvl], cgs.at[lvl], x_far),
        send(cgs.at[lvl], cgs.at[lvl], mate),
        send(cgs.at[lvl], cgs.at[lvl], cross),
    ]

    o_copies[0].wait_recv()
    o_mid[...] = (opart[:, far_frames, :].astype(F32) + o_core[0].astype(F32)).astype(BF16)
    o_far = send(o_mid, o_x, x_far)

    g_pass = []
    for k in range(2):
        g_up[k].wait_recv()
        g_pass.append(send(eg.at[k, FR : 2 * FR], eg.at[k, 3 * FR : 4 * FR], y_up))
    for k in range(2, 4):
        g_down[k].wait_recv()
        g_pass.append(send(eg.at[k, 2 * FR : 3 * FR], eg.at[k, 3 * FR : 4 * FR], y_down))

    for copy in cg_copies:
        copy.wait_recv()
    whole = jnp.concatenate([cgs[b] for b in range(4)], axis=1)
    hg_ref[...] = dot_nt(whole, win[...]).astype(BF16)

    def packed(xx, zz, k):
        return grads[k, block_rows(xx, zz), :]

    up_steps = [[], [], [], []]
    down_steps = [[], [], []]
    for t in range(4):
        for k in range(LV):
            if t == 0:
                if k < 2:
                    g_down[k].wait_recv()
                else:
                    g_up[k].wait_recv()
                g_pass[k].wait_recv()
                grads[k] = dot(oht[k], eg[k])
            if t > 0:
                up_steps[t - 1][k].wait_recv()
            for j in range(2):
                value = packed(xl if j == 0 else 1 - xl, z + 4 - t, k)
                if t > 0:
                    value = value + zs_recv[0, t - 1, k, j].astype(F32)
                zs_send[0, t, k, j] = value.astype(BF16)
            up_steps[t].append(send(zs_send.at[0, t, k], zs_recv.at[0, t, k], z_up))
            if t < 3:
                if t > 0:
                    down_steps[t - 1][k].wait_recv()
                for j in range(2):
                    value = packed(xl if j == 0 else 1 - xl, z - 3 + t, k)
                    if t > 0:
                        value = value + zs_recv[1, t - 1, k, j].astype(F32)
                    zs_send[1, t, k, j] = value.astype(BF16)
                down_steps[t].append(send(zs_send.at[1, t, k], zs_recv.at[1, t, k], z_down))

    o_copies[1].wait_recv()
    o_far.wait_recv()
    for k in range(LV):
        base = jnp.concatenate([streams[b, k, own_frames, :] for b in range(4)], axis=1).astype(F32)
        out_ref[k] = (
            base + opart[k, own_frames, :].astype(F32) + o_core[1, k].astype(F32) + o_x[k].astype(F32)
        ).astype(BF16)

    last = []
    for k in range(LV):
        up_steps[3][k].wait_recv()
        down_steps[2][k].wait_recv()
        value = (
            packed(1 - xl, z, k) + zs_recv[0, 3, k, 1].astype(F32) + zs_recv[1, 2, k, 1].astype(F32)
        )
        xs_send[k] = value.astype(BF16)
        last.append(send(xs_send.at[k], xs_recv.at[k], x_near))
    for k in range(LV):
        value = (
            packed(xl, z, k) + zs_recv[0, 3, k, 0].astype(F32) + zs_recv[1, 2, k, 0].astype(F32)
        )
        last[k].wait_recv()
        tg_ref[k] = value + xs_recv[k].astype(F32)

    for copy in started:
        copy.wait_send()


def shards(
    hidden, code_ids, lengths, weight_in, weight_query, weight_key, weight_value, weight_out,
    norm_gain, tables, upstream,
):
    codes = jnp.pad(code_ids.T, ((0, 8 - LV), (0, 0)))
    vmem = pl.BlockSpec(memory_space=pltpu.VMEM)
    hbm = pl.BlockSpec(memory_space=pl.ANY)
    smem = pl.BlockSpec(memory_space=pltpu.SMEM)

    def scratch(dtype, *shape):
        return pltpu.VMEM(shape, dtype)

    pairs = len(PAIRS)
    block = (LV, FR, COLS)
    out, hidden_grad, table_grad = pl.pallas_call(
        kernel,
        out_shape=(
            jax.ShapeDtypeStruct((LV, OWN, WIDTH), BF16),
            jax.ShapeDtypeStruct((FR, WIDTH), BF16),
            jax.ShapeDtypeStruct((LV, ENT, COLS), F32),
        ),
        in_specs=[vmem, smem, vmem, vmem, vmem, vmem, hbm, hbm, hbm, hbm, hbm],
        out_specs=(vmem, vmem, vmem),
        scratch_shapes=[
            scratch(BF16, WIDTH, WIDTH),
            scratch(BF16, WIDTH, COLS),
            scratch(BF16, WIDTH, COLS),
            scratch(BF16, WIDTH, COLS),
            scratch(BF16, COLS, WIDTH),
            scratch(jnp.int32, 8, FR),
            scratch(jnp.int32, NY, 8, FR),
            scratch(BF16, LV, RANGE, COLS),
            scratch(BF16, LV, NY * FR, RANGE),
            scratch(BF16, LV, RANGE, NY * FR),
            scratch(BF16, LV, FR, WIDTH),
            scratch(BF16, 4, FR, COLS),
            scratch(BF16, 3, FR, COLS),
            scratch(BF16, NY, *block),
            scratch(BF16, 2, 2, FR, COLS),
            scratch(BF16, 2, *block),
            scratch(F32, *block),
            scratch(BF16, 4, *block),
            scratch(BF16, LV, FR, WIDTH),
            scratch(F32, LV, FR, 128),
            scratch(BF16, *block),
            scratch(BF16, *block),
            scratch(BF16, *block),
            scratch(BF16, *block),
            scratch(BF16, 2 * pairs, FR, COLS),
            scratch(F32, 2 * pairs, FR, COLS),
            scratch(BF16, *block),
            scratch(BF16, *block),
            scratch(BF16, *block),
            scratch(BF16, *block),
            scratch(BF16, 3, *block),
            scratch(F32, *block),
            scratch(BF16, 2, *block),
            scratch(BF16, *block),
            scratch(BF16, *block),
            scratch(F32, LV, FR, 128),
            scratch(F32, 4, 8, FR),
            scratch(F32, LV, FR, 128),
            scratch(BF16, LV, FR, WIDTH),
            scratch(BF16, 2, LV, OWN, WIDTH),
            scratch(BF16, LV, OWN, WIDTH),
            scratch(BF16, LV, OWN, WIDTH),
            scratch(BF16, LV, NY * FR, COLS),
            scratch(BF16, 4, FR, COLS),
            scratch(F32, LV, RANGE, COLS),
            scratch(BF16, 2, 4, LV, 2, ENT, COLS),
            scratch(BF16, 2, 4, LV, 2, ENT, COLS),
            scratch(BF16, LV, ENT, COLS),
            scratch(BF16, LV, ENT, COLS),
            pltpu.SemaphoreType.DMA((5,)),
            pltpu.SemaphoreType.DMA((128,)),
            pltpu.SemaphoreType.DMA((128,)),
        ],
        compiler_params=pltpu.CompilerParams(
            collective_id=0, has_side_effects=True, vmem_limit_bytes=50 << 20
        ),
        name="layer",
    )(
        codes,
        lengths,
        norm_gain.reshape(1, WIDTH),
        jnp.transpose(tables, (1, 0, 2)),
        jnp.transpose(upstream, (1, 0, 2)),
        hidden,
        weight_in,
        weight_query,
        weight_key,
        weight_value,
        weight_out,
    )
    return (
        jnp.transpose(out, (1, 0, 2)),
        hidden_grad,
        jnp.transpose(table_grad, (1, 0, 2)),
    )


def solution(mesh):
    placed = (
        P("seq", "lvl"),
        P("seq", None),
        P(),
        P("lvl", None),
        P(None, "lvl"),
        P(None, "lvl"),
        P(None, "lvl"),
        P("lvl", None),
        P(),
        P("seq", None, "lvl"),
        P(("seq", "lvl"), None, None),
    )
    return jax.shard_map(
        shards,
        mesh=mesh,
        in_specs=placed,
        out_specs=(P(("seq", "lvl"), None, None), P("seq", "lvl"), P("seq", None, "lvl")),
        check_vma=False,
    )
```

time: 1130 us -> 107 us (0.09)
  waiting for transfers between devices: 1010 us -> 0 us
  Pallas kernels: 0 us -> 93.4 us
  matrix products: 55.2 us -> 0 us
  local copies, waits for them, and re-layouts: 31 us -> 11.4 us
  between operations: 16.4 us -> 0.66 us
    unnamed x8 -> x0, waiting for transfers between devices: 611 us -> none
    all_gather x3 -> x0, waiting for transfers between devices: 336 us -> none  [the longest x1 299 us: shards(): portion = lax.all_gather(tables, 'seq', axis=0, tiled=True)]
    pallas_call x0 -> x1, Pallas kernels: none -> 93.4 us  [shards(): pl.pallas_call(kernel, out_shape=(jax.ShapeDtypeStruct((LV, OWN, WIDTH),...]
    dot_general x17 -> x0, matrix products: 51.5 us -> none  [the longest x1 4.62 us: shards(): jnp.einsum('flr,flc->rlc', choose, embed_grad, preferred_element_type=jnp...]
    psum x2 -> x0, waiting for transfers between devices: 43.8 us -> none  [the longest x1 43.8 us: shards(): lax.psum(partial_normed.astype(jnp.bfloat16), 'lvl').astype(jnp.float32)]
    reduce_scatter x1 -> x0, waiting for transfers between devices: 17.8 us -> none  [shards(): lax.psum_scatter(jnp.einsum('flc,cd->fld', mixture, weight_out, preferred...]
  transfers between devices with their start and end apart: 8 -> 0, of which waited for: 7 -> 0; matrix products, arithmetic and copies ran while one was open for 4% -> 0% of each run, Pallas kernels for 0% -> 0%
where the time goes in v1:
time: 107 us; the launch traced here: 105 us
  Pallas kernels  93.4 us (87%)
  local copies, waits for them, and re-layouts  11.4 us (11%)
    pallas_call x1, Pallas kernels, shards(): pl.pallas_call(kernel, out_shape=(jax.ShapeDtypeStruct((LV, OWN, WIDTH),...  93.4 us
    unnamed x19, local copies, waits for them, and re-layouts  10.7 us

profile of v1, /device:TPU:4, one launch (start us, length us, event | category | flops | bytes accessed | tf_op | source)
XLA Modules:
  0.0 105.5 jit_solution(9265759333326490479)
XLA Ops:
  0.6 0.7 pad.4.codes_ref
  1.3 0.8 copy.21
  2.2 1.0 copy.20
  3.2 0.0 copy-start
  3.2 1.0 copy-done
  4.2 0.0 copy-start.1
  4.3 1.0 copy-done.1
  5.3 0.0 copy-start.2
  5.3 1.0 copy-done.2
  6.3 0.0 copy-start.3
  6.3 1.0 copy-done.3
  7.4 0.0 copy-start.4
  7.4 0.9 copy-done.4
  8.3 0.0 copy-start.5
  8.3 0.7 copy-done.5
  9.0 0.0 copy-start.6
  9.0 0.7 copy-done.6
  9.7 93.4 %layer.1 = (bf16[4,32,1024]{2,1,0:T(8,128)(2,1)S(1)}, bf16[128,1024]{1,0:T(8,128)(2,1)S(1)}, f32[4,32,256]{2,1,0:T(8,128)S(1)}) custom-call(s32[8,128]{1,0:T(8,128)S(1)} %pad.4.codes_ref, s32[4]{0:T(128)S(1)} %copy-done.6, f32[1,1024]{1,0:T(1,128)S(1)} %bitcast.14, bf16[4,32,256]{2,1,0:T(8,128)(2,1)S(1)} %bitcast.11, bf16[4,32,1024]{2,1,0:T(8,128)(2,1)S(1)} %bitcast.10, ...), custom_call_target="tpu_custom_call" | custom-call | tf_op jit(solution)/shard_map/layer/pallas_call | solution.py:505
  103.1 0.9 copy.16
  104.0 0.7 copy.17
  104.8 0.7 copy.23
Async XLA Ops:
  3.2 1.0 copy-start
  4.2 1.0 copy-start.1
  5.3 1.0 copy-start.2
  6.3 1.0 copy-start.3
  7.4 0.9 copy-start.4
  8.3 0.7 copy-start.5
  9.0 0.7 copy-start.6

commit v2 on v1

v2 whole, which is shorter than its diff:
```python
import math

import jax
import jax.numpy as jnp
from jax import lax
from jax.experimental import pallas as pl
from jax.experimental.pallas import tpu as pltpu
from jax.sharding import PartitionSpec as P

HEADS = 16
EPSILON = 1e-05
MESH = pl.DeviceIdType.MESH
F32 = jnp.float32
BF16 = jnp.bfloat16

NY, NZ = 4, 8
LV = 4
FR = 128
OWN = 32
COLS = 256
WIDTH = 1024
ENT = 32
RANGE = 512
COPIES = 192


def dot(a, b):
    return lax.dot_general(a, b, (((1,), (0,)), ((), ())), preferred_element_type=F32)


def dot_nt(a, b):
    return lax.dot_general(a, b, (((1,), (1,)), ((), ())), preferred_element_type=F32)


def kernel(
    codes_hbm, lens_hbm, gain_hbm, tab_hbm, up_hbm, hid_hbm, win_hbm, wq_hbm, wk_hbm, wv_hbm, wo_hbm,
    out_ref, hg_ref, tg_ref,
    codes_ref, lens_ref, gain_ref, hid_ref, win, wq, wk, wv, wo,
    nbr, prev, tab, oh, oht, ups, ctx_send, ctx_core, ctx_mid, ctx_x,
    look, relay, fin, stream_own, streams, normed, scale,
    qs, ks, vs, gms, prod, sums, mix, gqs, gks, gvs, gk_sum, gv_sum,
    pn, pn_own, pn_core, pn_mid, pn_x, stat_wide, stat, stat_col,
    opart, o_core, o_mid, o_x,
    eg, cgs, grads, f3_send, f3_recv, f4_send, f4_recv, c1_send, c1_recv, c2_send, c2_recv, d_send, d_recv,
    local_sem, ssem, rsem,
):
    seq = lax.axis_index("seq")
    lvl = lax.axis_index("lvl")
    y = lax.div(seq, 16)
    xl = lax.rem(lax.div(seq, 8), 2)
    z = lax.rem(seq, 8)
    xh = lax.div(lvl, 2)
    core = lax.rem(lvl, 2)

    def device(dy=0, dx=0, dz=0, dh=0, dc=0):
        yy = lax.rem(y + dy + NY, NY)
        xx = 1 - xl if dx else xl
        zz = lax.rem(z + dz + NZ, NZ)
        hh = 1 - xh if dh else xh
        cc = 1 - core if dc else core
        return (yy * 16 + xx * 8 + zz, hh * 2 + cc)

    seq_next = (lax.rem(seq + 1, 64), lvl)
    seq_back = (lax.rem(seq + 63, 64), lvl)
    y_up, y_down, y_far = device(dy=1), device(dy=-1), device(dy=2)
    z_up, z_down, z_up2, z_down2 = device(dz=1), device(dz=-1), device(dz=2), device(dz=-2)
    x_near, x_far, mate, cross = device(dx=1), device(dh=1), device(dc=1), device(dh=1, dc=1)
    lvl_far = (1 - xh) * 2 + core
    lvl_mate = xh * 2 + 1 - core
    lvl_cross = (1 - xh) * 2 + 1 - core

    started = []

    def send(src, dst, target):
        i = len(started)
        copy = pltpu.make_async_remote_copy(
            src_ref=src, dst_ref=dst, send_sem=ssem.at[i], recv_sem=rsem.at[i],
            device_id=target, device_id_type=MESH,
        )
        copy.start()
        started.append(copy)
        return copy

    def push(ref, target):
        return send(ref, ref, target)

    def rows(start, size):
        return pl.ds(pl.multiple_of(start, size), size)

    def block_rows(xx, zz):
        return rows((xx * 8 + lax.rem(zz + NZ, NZ)) * ENT, ENT)

    own_rows = block_rows(xl, z)
    own_frames = rows(lvl * OWN, OWN)
    far_frames = rows(lvl_far * OWN, OWN)
    mate_frames = rows(lvl_mate * OWN, OWN)
    cross_frames = rows(lvl_cross * OWN, OWN)

    codes_ref[...] = jnp.zeros((8, FR), jnp.int32)
    fetch = {}
    for i, (name, a, b) in enumerate(
        (
            ("tab", tab_hbm, tab.at[:, own_rows]),
            ("codes", codes_hbm, codes_ref.at[0:LV]),
            ("hid", hid_hbm, hid_ref),
            ("win", win_hbm, win),
            ("ups", up_hbm, ups.at[:, own_frames]),
            ("lens", lens_hbm, lens_ref),
            ("gain", gain_hbm, gain_ref),
            ("wo", wo_hbm, wo),
            ("wq", wq_hbm, wq),
            ("wk", wk_hbm, wk),
            ("wv", wv_hbm, wv),
        )
    ):
        fetch[name] = pltpu.make_async_copy(a, b, local_sem.at[i])
        fetch[name].start()

    barrier = pltpu.get_barrier_semaphore()
    for source in (z_up, z_down, z_up2, z_down2, x_near, y_up, y_down, y_far, mate, x_far, cross, seq_back):
        pl.semaphore_signal(barrier, inc=1, device_id=source, device_id_type=MESH)
    fetch["hid"].wait()
    fetch["win"].wait()
    part = dot(hid_ref[...], win[...])
    for b in range(4):
        ctx_send[b] = part[:, b * COLS : (b + 1) * COLS].astype(BF16)
    fetch["tab"].wait()
    fetch["codes"].wait()
    pl.semaphore_wait(barrier, 12)

    def block(half, xx, zz):
        return tab.at[2 * half : 2 * half + 2, block_rows(xx, zz)]

    own = [block(h, xl, z) for h in range(2)]
    up2, down2, up1, down1, near_own = [], [], [], [], []
    for h in range(2):
        up2.append(push(own[h], z_up2))
        down2.append(push(own[h], z_down2))
        near_own.append(push(own[h], x_near))
        up1.append(push(own[h], z_up))
        down1.append(push(own[h], z_down))
    code_copy = send(codes_ref, nbr, seq_next)
    ctx_copies = [
        send(ctx_send.at[lvl_cross], ctx_core.at[0], mate),
        send(ctx_send.at[lvl_mate], ctx_core.at[1], mate),
    ]
    fetch["ups"].wait()
    up_mate = [push(ups.at[k, own_frames], mate) for k in range(LV)]

    near2, up3, down3, near1 = [], [], [], []
    for h in range(2):
        up2[h].wait_recv()
        near2.append(push(block(h, xl, z - 2), x_near))
        up3.append(push(block(h, xl, z - 2), z_up))
        if h == 0:
            end_up = push(block(0, xl, z - 2), z_up2)
        down2[h].wait_recv()
        near2.append(push(block(h, xl, z + 2), x_near))
        down3.append(push(block(h, xl, z + 2), z_down))
        if h == 1:
            end_down = push(block(1, xl, z + 2), z_down2)
    for h in range(2):
        up1[h].wait_recv()
        near1.append(push(block(h, xl, z - 1), x_near))
        down1[h].wait_recv()
        near1.append(push(block(h, xl, z + 1), x_near))

    code_copy.wait_recv()
    lane8 = lax.broadcasted_iota(jnp.int32, (8, FR), 1)
    sub8 = lax.broadcasted_iota(jnp.int32, (8, FR), 0)
    own_codes = codes_ref[...]
    shifted = pltpu.roll(own_codes, 1, 1)
    incoming = pltpu.roll(nbr[...], 1, 1)
    incoming = jnp.where(jnp.broadcast_to(seq, (8, FR)) == 0, 0, incoming)
    shifted = jnp.where(lane8 == 0, incoming, shifted)
    first_row = jnp.broadcast_to(shifted[LV - 1 : LV, :], (8, FR))
    prev[0] = jnp.where(sub8 == 0, first_row, pltpu.roll(own_codes, 1, 0))
    code_y = [
        send(prev.at[0], prev.at[1], y_up),
        send(prev.at[0], prev.at[2], y_down),
        send(prev.at[0], prev.at[3], y_far),
    ]
    ctx_copies[0].wait_recv()
    ctx_mid[...] = (ctx_send[lvl_far].astype(F32) + ctx_core[0].astype(F32)).astype(BF16)
    ctx_far = send(ctx_mid, ctx_x, x_far)

    for copy in code_y:
        copy.wait_recv()
    first = y * RANGE
    by_lane = lax.broadcasted_iota(jnp.int32, (FR, RANGE), 1) + first
    by_row = lax.broadcasted_iota(jnp.int32, (RANGE, FR), 0) + first
    for slot in range(NY):
        codes = prev[slot]
        turned = jnp.transpose(
            jnp.concatenate([codes.astype(F32), jnp.zeros((FR - 8, FR), F32)], axis=0)
        ).astype(jnp.int32)
        for k in range(LV):
            column = jnp.broadcast_to(turned[:, k : k + 1], (FR, RANGE))
            oh[k, slot * FR : (slot + 1) * FR, :] = jnp.where(column == by_lane, 1.0, 0.0).astype(BF16)

    far_up, far_down = [], []
    for h in range(2):
        near2[2 * h].wait_recv()
        far_up.append(push(block(h, 1 - xl, z - 2), z_up))
        if h == 0:
            far_end_up = push(block(0, 1 - xl, z - 2), z_up2)
        near2[2 * h + 1].wait_recv()
        far_down.append(push(block(h, 1 - xl, z + 2), z_down))
        if h == 1:
            far_end_down = push(block(1, 1 - xl, z + 2), z_down2)
    up_far = [push(ups.at[k, own_frames], x_far) for k in range(LV)]

    for slot in range(NY):
        codes = prev[slot]
        for k in range(LV):
            row = jnp.broadcast_to(codes[k : k + 1, :], (RANGE, FR))
            oht[k, :, slot * FR : (slot + 1) * FR] = jnp.where(row == by_row, 1.0, 0.0).astype(BF16)
    fetch["lens"].wait()
    frame = lax.broadcasted_iota(jnp.int32, (FR, COLS), 0) + seq * FR
    begin = jnp.int32(0)
    retain = jnp.ones((FR, COLS), F32)
    for i in range(4):
        retain = jnp.where(frame == begin, 0.0, retain)
        begin = begin + lens_ref[i]
    ctx_copies[1].wait_recv()
    ctx_far.wait_recv()
    context = ctx_send[lvl].astype(F32) + ctx_core[1].astype(F32) + ctx_x[...].astype(F32)

    top, low = slice(0, FR // 2), slice(FR // 2, FR)
    relay_up, relay_down = [], []
    fin_up = [[None, None] for _ in range(LV)]
    fin_down = [[None, None] for _ in range(LV)]

    def find(k):
        found = dot(oh[k], tab[k]).astype(BF16)
        for slot in (3, 2, 1, 0):
            look[slot, k] = found[slot * FR : (slot + 1) * FR, :]
        relay_up.append(send(look.at[3, k, top], relay.at[0, k], y_up))
        relay_down.append(send(look.at[3, k, low], relay.at[1, k], y_down))

    def direct(k):
        fin_up[k][1] = send(look.at[2, k, low], fin.at[0, k, low], y_up)
        fin_down[k][0] = send(look.at[1, k, top], fin.at[1, k, top], y_down)

    def relayed(k):
        relay_up[k].wait_recv()
        look[2, k, top] = look[2, k, top] + relay[0, k]
        fin_up[k][0] = send(look.at[2, k, top], fin.at[0, k, top], y_up)
        relay_down[k].wait_recv()
        look[1, k, low] = look[1, k, low] + relay[1, k]
        fin_down[k][1] = send(look.at[1, k, low], fin.at[1, k, low], y_down)

    far, near, passed = [], [], []

    def stream(k):
        for copy in fin_up[k] + fin_down[k]:
            copy.wait_recv()
        embedded = look[0, k].astype(F32) + fin[0, k].astype(F32) + fin[1, k].astype(F32)
        if k == 0:
            embedded = retain * embedded
        own = context + embedded
        stream_own[k] = own
        streams[lvl, k] = own.astype(BF16)
        far.append(push(streams.at[lvl, k], x_far))
        near.append(push(streams.at[lvl, k], mate))

    def pass_stream(k):
        far[k].wait_recv()
        passed.append(push(streams.at[lvl_far, k], mate))

    def blocks_in(h):
        for copy in (up3[h], down3[h], near_own[h], near1[2 * h], near1[2 * h + 1], far_up[h], far_down[h]):
            copy.wait_recv()

    blocks_in(0)
    end_up.wait_recv()
    far_end_up.wait_recv()
    find(0)
    find(1)
    direct(0)
    blocks_in(1)
    end_down.wait_recv()
    far_end_down.wait_recv()
    find(2)
    find(3)
    direct(1)
    relayed(0)
    relayed(1)
    direct(2)
    relayed(2)
    direct(3)
    relayed(3)
    stream(0)
    stream(1)
    stream(2)
    stream(3)
    up_pass = []
    for k in range(LV):
        up_far[k].wait_recv()
        up_pass.append(push(ups.at[k, far_frames], mate))
    pass_stream(0)
    pass_stream(1)
    fetch["wo"].wait()
    for k in range(LV):
        up_mate[k].wait_recv()
        up_pass[k].wait_recv()
    gms[...] = dot_nt(ups[...].reshape(LV * FR, WIDTH), wo[...]).astype(BF16).reshape(LV, FR, COLS)
    for name in ("gain", "wq", "wk", "wv"):
        fetch[name].wait()

    head_row = lax.shift_right_logical(lax.broadcasted_iota(jnp.int32, (COLS, COLS), 0), 6)
    head_col = lax.shift_right_logical(lax.broadcasted_iota(jnp.int32, (COLS, COLS), 1), 6)
    same_head = jnp.where(head_row == head_col, 1.0, 0.0).astype(BF16)
    scaling = 1.0 / math.sqrt(WIDTH // HEADS)

    def norm(a):
        near[a].wait_recv()
        passed[a].wait_recv()

        def norm_body(i, carry):
            r = rows(i * 32, 32)
            blocks = [streams[b, a, r, :].astype(F32) for b in range(4)]
            total = blocks[0] * blocks[0]
            for b in range(1, 4):
                total = total + blocks[b] * blocks[b]
            scaler = lax.rsqrt(jnp.sum(total, axis=1, keepdims=True) * (1.0 / WIDTH) + EPSILON)
            scale[a, r, :] = jnp.broadcast_to(scaler, (32, 128))
            for b in range(4):
                normed[a, r, b * COLS : (b + 1) * COLS] = (
                    blocks[b] * scaler * gain_ref[:, b * COLS : (b + 1) * COLS]
                ).astype(BF16)
            return carry

        lax.fori_loop(0, 4, norm_body, 0)

    def attend_level(a, base):
        def attend_body(i, carry):
            r = rows(lax.div(i, 2) * 16, 16)
            c = rows(lax.rem(i, 2) * 128, 128)
            q = qs[a, r, c].astype(F32)
            g = gms[a, r, c].astype(F32)
            raised = [jnp.exp(sums[base + b, r, c] * scaling) for b in range(a + 1)]
            total = raised[0]
            for b in range(1, a + 1):
                total = total + raised[b]
            inverse = 1.0 / total
            weights = [x * inverse for x in raised]
            rounded = [x.astype(BF16).astype(F32) for x in weights]
            slopes = [sums[base + a + 1 + b, r, c] for b in range(a + 1)]
            mixed = rounded[0] * vs[0, r, c].astype(F32)
            mean = weights[0] * slopes[0]
            for b in range(1, a + 1):
                mixed = mixed + rounded[b] * vs[b, r, c].astype(F32)
                mean = mean + weights[b] * slopes[b]
            mix[a, r, c] = mixed.astype(BF16)
            grad_query = None
            for b in range(a + 1):
                grad_score = (weights[b] * (slopes[b] - mean) * scaling).astype(BF16).astype(F32)
                term_q = grad_score * ks[b, r, c].astype(F32)
                term_k = grad_score * q
                term_v = rounded[b] * g
                grad_query = term_q if b == 0 else grad_query + term_q
                if a > b:
                    term_k = term_k + gk_sum[b, r, c]
                    term_v = term_v + gv_sum[b, r, c]
                if a == LV - 1:
                    gks[b, r, c] = term_k.astype(BF16)
                    gvs[b, r, c] = term_v.astype(BF16)
                else:
                    gk_sum[b, r, c] = term_k
                    gv_sum[b, r, c] = term_v
            gqs[a, r, c] = grad_query.astype(BF16)
            return carry

        lax.fori_loop(0, 16, attend_body, 0)

    def two_levels(first):
        x = normed[first : first + 2].reshape(2 * FR, WIDTH)
        for w, target in ((wq, qs), (wk, ks), (wv, vs)):
            target[first : first + 2] = dot(x, w[...]).astype(BF16).reshape(2, FR, COLS)
        count = 2 * (first + 1) + 2 * (first + 2)

        def product_body(i, carry):
            r = rows(i * 16, 16)
            base = 0
            for a in (first, first + 1):
                q = qs[a, r, :].astype(F32)
                g = gms[a, r, :].astype(F32)
                for b in range(a + 1):
                    prod[base + b, r, :] = (q * ks[b, r, :].astype(F32)).astype(BF16)
                    prod[base + a + 1 + b, r, :] = (g * vs[b, r, :].astype(F32)).astype(BF16)
                base += 2 * (a + 1)
            return carry

        lax.fori_loop(0, 8, product_body, 0)
        sums[0:count] = dot(prod[0:count].reshape(count * FR, COLS), same_head).reshape(count, FR, COLS)
        attend_level(first, 0)
        attend_level(first + 1, 2 * (first + 1))

    norm(0)
    norm(1)
    pass_stream(2)
    two_levels(0)
    norm(2)
    pass_stream(3)
    norm(3)
    two_levels(2)

    def stat_body(i, carry):
        r = rows(i * 32, 32)
        for k in range(LV):
            share = (
                qs[k, r, :].astype(F32) * gqs[k, r, :].astype(F32)
                + ks[k, r, :].astype(F32) * gks[k, r, :].astype(F32)
                + vs[k, r, :].astype(F32) * gvs[k, r, :].astype(F32)
            )
            stat_wide[k, r, :] = jnp.broadcast_to(jnp.sum(share, axis=1, keepdims=True), (32, 128))
        return carry

    lax.fori_loop(0, 4, stat_body, 0)
    eye = lax.broadcasted_iota(jnp.int32, (FR, FR), 0) == lax.broadcasted_iota(jnp.int32, (FR, FR), 1)
    for k in range(LV):
        stat[0, k : k + 1, :] = jnp.sum(jnp.where(eye, stat_wide[k], 0.0), axis=0, keepdims=True)
    stat[0, LV:, :] = jnp.zeros((8 - LV, FR), F32)
    stat_copies = [
        send(stat.at[0], stat.at[1], x_far),
        send(stat.at[0], stat.at[2], mate),
        send(stat.at[0], stat.at[3], cross),
    ]

    gq = gqs[...].reshape(LV * FR, COLS)
    gk = gks[...].reshape(LV * FR, COLS)
    gv = gvs[...].reshape(LV * FR, COLS)

    def partial(owner):
        w = rows(owner * COLS, COLS)
        total = dot_nt(gq, wq[w, :]) + dot_nt(gk, wk[w, :]) + dot_nt(gv, wv[w, :])
        return total.reshape(LV, FR, COLS)

    pn[0] = partial(lvl_cross).astype(BF16)
    pn_cross = [send(pn.at[0, k], pn_core.at[0, k], mate) for k in range(LV)]
    pn[2] = partial(lvl_far).astype(BF16)
    pn_far = []
    for k in range(LV):
        pn_cross[k].wait_recv()
        pn_mid[k] = (pn[2, k].astype(F32) + pn_core[0, k].astype(F32)).astype(BF16)
        pn_far.append(send(pn_mid.at[k], pn_x.at[k], x_far))
    pn[1] = partial(lvl_mate).astype(BF16)
    pn_mate = [send(pn.at[1, k], pn_core.at[1, k], mate) for k in range(LV)]
    opart[...] = dot(mix[...].reshape(LV * FR, COLS), wo[...]).astype(BF16).reshape(LV, FR, WIDTH)
    o_copies = [
        send(opart.at[:, cross_frames], o_core.at[0], mate),
        send(opart.at[:, mate_frames], o_core.at[1], mate),
    ]
    pn_own[...] = partial(lvl)

    for copy in stat_copies:
        copy.wait_recv()
    stat_all = (stat[0] + stat[1] + stat[2] + stat[3]) * (1.0 / WIDTH)
    for k in range(LV):
        column = jnp.sum(
            jnp.where(eye, jnp.broadcast_to(stat_all[k : k + 1, :], (FR, FR)), 0.0), axis=1, keepdims=True
        )
        stat_col[k] = jnp.broadcast_to(column, (FR, 128))

    own_cols = rows(lvl * COLS, COLS)
    gain = gain_ref[:, own_cols]
    context_grads = []
    g_copies = []

    def stream_grad(k):
        pn_mate[k].wait_recv()
        pn_far[k].wait_recv()
        grad_normed = pn_own[k] + pn_core[1, k].astype(F32) + pn_x[k].astype(F32)
        scaler = scale[k][:, 0:1]
        unit = stream_own[k] * scaler
        grad = ups[k, :, own_cols].astype(F32) + scaler * (gain * grad_normed - unit * stat_col[k][:, 0:1])
        context_grads.append(grad)
        eg[k, 0:FR, :] = (retain * grad if k == 0 else grad).astype(BF16)
        copies = []
        if k == LV - 1:
            copies.append(send(eg.at[k, 0:FR], eg.at[k, 3 * FR : 4 * FR], y_far))
        copies.append(send(eg.at[k, 0:FR], eg.at[k, FR : 2 * FR], y_up))
        copies.append(send(eg.at[k, 0:FR], eg.at[k, 2 * FR : 3 * FR], y_down))
        g_copies.append(copies)

    def pass_grad(k):
        copy_up, copy_down = g_copies[k]
        copy_up.wait_recv()
        pass_up = send(eg.at[k, FR : FR + FR // 2], eg.at[k, 3 * FR : 3 * FR + FR // 2], y_up)
        copy_down.wait_recv()
        pass_down = send(
            eg.at[k, 2 * FR + FR // 2 : 3 * FR], eg.at[k, 3 * FR + FR // 2 : 4 * FR], y_down
        )
        g_copies[k] = [pass_up, pass_down]

    stream_grad(0)
    stream_grad(1)
    o_copies[0].wait_recv()
    o_mid[...] = (opart[:, far_frames, :].astype(F32) + o_core[0].astype(F32)).astype(BF16)
    stream_grad(2)
    o_far = send(o_mid, o_x, x_far)
    pass_grad(0)
    stream_grad(3)
    pass_grad(1)
    cgs[lvl] = (context_grads[0] + context_grads[1] + context_grads[2] + context_grads[3]).astype(BF16)
    cg_far = push(cgs.at[lvl], x_far)
    cg_mate = push(cgs.at[lvl], mate)
    pass_grad(2)

    half = ENT // 2
    fringe, crossed, direct_sums = [], [], []

    def packed(xx, zz, k):
        return grads[k, block_rows(xx, zz), :]

    def fringe_step(k):
        for copy in g_copies[k]:
            copy.wait_recv()
        grads[k] = dot(oht[k], eg[k])
        for j, xx in enumerate((xl, 1 - xl)):
            f3_send[0, k, j] = packed(xx, z - 3, k).astype(BF16)
            f3_send[1, k, j] = packed(xx, z + 3, k).astype(BF16)
            value = packed(xx, z + 4, k).astype(BF16)
            f4_send[0, k, j] = value[0:half, :]
            f4_send[1, k, j] = value[half:, :]
        fringe.append(
            [
                send(f3_send.at[0, k], f3_recv.at[0, k], z_down),
                send(f3_send.at[1, k], f3_recv.at[1, k], z_up),
                send(f4_send.at[0, k], f4_recv.at[0, k], z_down2),
                send(f4_send.at[1, k], f4_recv.at[1, k], z_up2),
            ]
        )
        for o in range(3):
            c1_send[k, o] = packed(1 - xl, z + o - 1, k).astype(BF16)
        crossed.append([send(c1_send.at[k], c1_recv.at[k], x_near)])

    def two_away(side, j, k):
        value = packed(xl if j == 0 else 1 - xl, z - 2 if side == 0 else z + 2, k)
        value = value + f3_recv[side, k, j].astype(F32)
        ends = f4_recv[side, k, j].astype(F32)
        zeros = jnp.zeros((half, COLS), F32)
        return value + jnp.concatenate([ends, zeros] if side == 0 else [zeros, ends], axis=0)

    def cross_step(k):
        for copy in fringe[k]:
            copy.wait_recv()
        for side in range(2):
            c2_send[k, side] = two_away(side, 1, k).astype(BF16)
        crossed[k].append(send(c2_send.at[k], c2_recv.at[k], x_near))

    def direct_step(k):
        for copy in crossed[k]:
            copy.wait_recv()
        for side in range(2):
            value = two_away(side, 0, k) + c2_recv[k, side].astype(F32)
            d_send[2 + side, k] = value.astype(BF16)
            value = packed(xl, z + 2 * side - 1, k) + c1_recv[k, 2 * side].astype(F32)
            d_send[side, k] = value.astype(BF16)
        direct_sums.append(
            [
                send(d_send.at[i, k], d_recv.at[i, k], target)
                for i, target in ((2, z_down2), (3, z_up2), (0, z_down), (1, z_up))
            ]
        )

    def final_step(k):
        value = packed(xl, z, k) + c1_recv[k, 1].astype(F32)
        for copy in direct_sums[k]:
            copy.wait_recv()
        for i in range(4):
            value = value + d_recv[i, k].astype(F32)
        tg_ref[k] = value

    fringe_step(0)
    fringe_step(1)
    fringe_step(2)
    fringe_step(3)
    cross_step(0)
    cross_step(1)
    direct_step(0)
    cross_step(2)
    cross_step(3)
    cg_far.wait_recv()
    cg_pass = push(cgs.at[lvl_far], mate)
    direct_step(1)
    direct_step(2)
    direct_step(3)

    cg_mate.wait_recv()
    cg_pass.wait_recv()
    whole = jnp.concatenate([cgs[b] for b in range(4)], axis=1)
    hg_ref[...] = dot_nt(whole, win[...]).astype(BF16)

    o_copies[1].wait_recv()
    o_far.wait_recv()
    for k in range(LV):
        base = jnp.concatenate([streams[b, k, own_frames, :] for b in range(4)], axis=1).astype(F32)
        out_ref[k] = (
            base + opart[k, own_frames, :].astype(F32) + o_core[1, k].astype(F32) + o_x[k].astype(F32)
        ).astype(BF16)
    for k in range(LV):
        final_step(k)

    for copy in started:
        copy.wait_send()
    assert len(started) <= COPIES


def shards(
    hidden, code_ids, lengths, weight_in, weight_query, weight_key, weight_value, weight_out,
    norm_gain, tables, upstream,
):
    vmem = pl.BlockSpec(memory_space=pltpu.VMEM)
    hbm = pl.BlockSpec(memory_space=pltpu.HBM)

    def scratch(dtype, *shape):
        return pltpu.VMEM(shape, dtype)

    block = (LV, FR, COLS)
    out, hidden_grad, table_grad = pl.pallas_call(
        kernel,
        out_shape=(
            jax.ShapeDtypeStruct((LV, OWN, WIDTH), BF16),
            jax.ShapeDtypeStruct((FR, WIDTH), BF16),
            jax.ShapeDtypeStruct((LV, ENT, COLS), F32),
        ),
        in_specs=[hbm] * 11,
        out_specs=(vmem, vmem, vmem),
        scratch_shapes=[
            scratch(jnp.int32, 8, FR),
            pltpu.SMEM((4,), jnp.int32),
            scratch(F32, 1, WIDTH),
            scratch(BF16, FR, WIDTH),
            scratch(BF16, WIDTH, WIDTH),
            scratch(BF16, WIDTH, COLS),
            scratch(BF16, WIDTH, COLS),
            scratch(BF16, WIDTH, COLS),
            scratch(BF16, COLS, WIDTH),
            scratch(jnp.int32, 8, FR),
            scratch(jnp.int32, NY, 8, FR),
            scratch(BF16, LV, RANGE, COLS),
            scratch(BF16, LV, NY * FR, RANGE),
            scratch(BF16, LV, RANGE, NY * FR),
            scratch(BF16, LV, FR, WIDTH),
            scratch(BF16, 4, FR, COLS),
            scratch(BF16, 2, FR, COLS),
            scratch(BF16, FR, COLS),
            scratch(BF16, FR, COLS),
            scratch(BF16, NY, *block),
            scratch(BF16, 2, LV, FR // 2, COLS),
            scratch(BF16, 2, *block),
            scratch(F32, *block),
            scratch(BF16, 4, *block),
            scratch(BF16, LV, FR, WIDTH),
            scratch(F32, LV, FR, 128),
            scratch(BF16, *block),
            scratch(BF16, *block),
            scratch(BF16, *block),
            scratch(BF16, *block),
            scratch(BF16, 14, FR, COLS),
            scratch(F32, 14, FR, COLS),
            scratch(BF16, *block),
            scratch(BF16, *block),
            scratch(BF16, *block),
            scratch(BF16, *block),
            scratch(F32, *block),
            scratch(F32, *block),
            scratch(BF16, 3, *block),
            scratch(F32, *block),
            scratch(BF16, 2, *block),
            scratch(BF16, *block),
            scratch(BF16, *block),
            scratch(F32, LV, FR, 128),
            scratch(F32, 4, 8, FR),
            scratch(F32, LV, FR, 128),
            scratch(BF16, LV, FR, WIDTH),
            scratch(BF16, 2, LV, OWN, WIDTH),
            scratch(BF16, LV, OWN, WIDTH),
            scratch(BF16, LV, OWN, WIDTH),
            scratch(BF16, LV, NY * FR, COLS),
            scratch(BF16, 4, FR, COLS),
            scratch(F32, LV, RANGE, COLS),
            scratch(BF16, 2, LV, 2, ENT, COLS),
            scratch(BF16, 2, LV, 2, ENT, COLS),
            scratch(BF16, 2, LV, 2, ENT // 2, COLS),
            scratch(BF16, 2, LV, 2, ENT // 2, COLS),
            scratch(BF16, LV, 3, ENT, COLS),
            scratch(BF16, LV, 3, ENT, COLS),
            scratch(BF16, LV, 2, ENT, COLS),
            scratch(BF16, LV, 2, ENT, COLS),
            scratch(BF16, 4, LV, ENT, COLS),
            scratch(BF16, 4, LV, ENT, COLS),
            pltpu.SemaphoreType.DMA((11,)),
            pltpu.SemaphoreType.DMA((COPIES,)),
            pltpu.SemaphoreType.DMA((COPIES,)),
        ],
        compiler_params=pltpu.CompilerParams(
            collective_id=0, has_side_effects=True, vmem_limit_bytes=53 << 20
        ),
        name="layer",
    )(
        code_ids.T,
        lengths,
        norm_gain.reshape(1, WIDTH),
        jnp.transpose(tables, (1, 0, 2)),
        jnp.transpose(upstream, (1, 0, 2)),
        hidden,
        weight_in,
        weight_query,
        weight_key,
        weight_value,
        weight_out,
    )
    return (
        jnp.transpose(out, (1, 0, 2)),
        hidden_grad,
        jnp.transpose(table_grad, (1, 0, 2)),
    )


def solution(mesh):
    placed = (
        P("seq", "lvl"),
        P("seq", None),
        P(),
        P("lvl", None),
        P(None, "lvl"),
        P(None, "lvl"),
        P(None, "lvl"),
        P("lvl", None),
        P(),
        P("seq", None, "lvl"),
        P(("seq", "lvl"), None, None),
    )
    return jax.shard_map(
        shards,
        mesh=mesh,
        in_specs=placed,
        out_specs=(P(("seq", "lvl"), None, None), P("seq", "lvl"), P("seq", None, "lvl")),
        check_vma=False,
    )
```

time: 107 us -> 88.1 us (0.82)
  Pallas kernels: 93.4 us -> 79.9 us
  local copies, waits for them, and re-layouts: 11.4 us -> 6.96 us
    pallas_call x1, Pallas kernels: 93.4 us -> 79.9 us  [shards(): pl.pallas_call(kernel, out_shape=(jax.ShapeDtypeStruct((LV, OWN, WIDTH),...]
    unnamed x19 -> x11, local copies, waits for them, and re-layouts: 10.7 us -> 6.96 us
where the time goes in v2:
time: 88.1 us; the launch traced here: 87.5 us
  Pallas kernels  79.9 us (91%)
  local copies, waits for them, and re-layouts  6.96 us (8%)
    pallas_call x1, Pallas kernels, shards(): pl.pallas_call(kernel, out_shape=(jax.ShapeDtypeStruct((LV, OWN, WIDTH),...  79.9 us
    unnamed x11, local copies, waits for them, and re-layouts  6.96 us

profile of v2, /device:TPU:4, one launch (start us, length us, event | category | flops | bytes accessed | tf_op | source)
XLA Modules:
  0.0 87.5 jit_solution(11386662589656523161)
XLA Ops:
  0.6 0.8 copy.21
  1.5 1.7 %copy.20 = bf16[32,4,1024]{2,0,1:T(8,128)(2,1)} copy(bf16[32,4,1024]{2,1,0:T(4,128)(2,1)} %param.21) | data formatting | bytes 524288 | tf_op args[10]
  3.2 0.0 copy-start
  3.2 0.7 copy-done
  3.9 0.0 copy-start.1
  3.9 0.7 copy-done.1
  4.6 0.0 copy-start.2
  4.6 0.7 copy-done.2
  5.2 79.9 %layer.1 = (bf16[4,32,1024]{2,1,0:T(8,128)(2,1)S(1)}, bf16[128,1024]{1,0:T(8,128)(2,1)S(1)}, f32[4,32,256]{2,1,0:T(8,128)S(1)}) custom-call(s32[4,128]{1,0:T(4,128)S(1)} %bitcast.14, s32[4]{0:T(128)S(1)} %copy-done.2, f32[1,1024]{1,0:T(1,128)S(1)} %bitcast.13, bf16[4,32,256]{2,1,0:T(8,128)(2,1)S(1)} %bitcast.10, bf16[4,32,1024]{2,1,0:T(8,128)(2,1)} %bitcast.15, ...), custom_call_target="tpu_custom_call" | custom-call | tf_op jit(solution)/shard_map/layer/pallas_call | solution.py:622
  85.1 0.9 %copy.16 = bf16[32,4,1024]{2,1,0:T(4,128)(2,1)} copy(bf16[32,4,1024]{2,0,1:T(8,128)(2,1)S(1)} %bitcast.11) | data formatting | bytes 524288
  86.0 0.7 copy.17
  86.8 0.7 copy.23
Async XLA Ops:
  3.2 0.7 copy-start
  3.9 0.7 copy-start.1
  4.6 0.7 copy-start.2

commit v3 on v2

--- a/solution.py
+++ b/solution.py
@@ -22,6 +22,7 @@
 ENT = 32
 RANGE = 512
 COPIES = 192
+VMEM_BYTES = 56 << 20
 
 
 def dot(a, b):
@@ -34,8 +35,9 @@
 
 def kernel(
     codes_hbm, lens_hbm, gain_hbm, tab_hbm, up_hbm, hid_hbm, win_hbm, wq_hbm, wk_hbm, wv_hbm, wo_hbm,
+    out_hbm, hg_hbm, tg_hbm,
     out_ref, hg_ref, tg_ref,
-    codes_ref, lens_ref, gain_ref, hid_ref, win, wq, wk, wv, wo,
+    tab_in, up_in, codes_ref, lens_ref, gain_ref, hid_ref, win, wq, wk, wv, wo,
     nbr, prev, tab, oh, oht, ups, ctx_send, ctx_core, ctx_mid, ctx_x,
     look, relay, fin, stream_own, streams, normed, scale,
     qs, ks, vs, gms, prod, sums, mix, gqs, gks, gvs, gk_sum, gv_sum,
@@ -100,11 +102,11 @@
     fetch = {}
     for i, (name, a, b) in enumerate(
         (
-            ("tab", tab_hbm, tab.at[:, own_rows]),
+            ("tab", tab_hbm, tab_in),
             ("codes", codes_hbm, codes_ref.at[0:LV]),
             ("hid", hid_hbm, hid_ref),
             ("win", win_hbm, win),
-            ("ups", up_hbm, ups.at[:, own_frames]),
+            ("ups", up_hbm, up_in),
             ("lens", lens_hbm, lens_ref),
             ("gain", gain_hbm, gain_ref),
             ("wo", wo_hbm, wo),
@@ -125,6 +127,8 @@
     for b in range(4):
         ctx_send[b] = part[:, b * COLS : (b + 1) * COLS].astype(BF16)
     fetch["tab"].wait()
+    for k in range(LV):
+        tab[k, own_rows, :] = tab_in[:, k, :]
     fetch["codes"].wait()
     pl.semaphore_wait(barrier, 12)
 
@@ -145,6 +149,8 @@
         send(ctx_send.at[lvl_mate], ctx_core.at[1], mate),
     ]
     fetch["ups"].wait()
+    for k in range(LV):
+        ups[k, own_frames, :] = up_in[:, k, :]
     up_mate = [push(ups.at[k, own_frames], mate) for k in range(LV)]
 
     near2, up3, down3, near1 = [], [], [], []
@@ -571,7 +577,7 @@
             copy.wait_recv()
         for i in range(4):
             value = value + d_recv[i, k].astype(F32)
-        tg_ref[k] = value
+        tg_ref[:, k, :] = value
 
     fringe_step(0)
     fringe_step(1)
@@ -592,43 +598,74 @@
     cg_pass.wait_recv()
     whole = jnp.concatenate([cgs[b] for b in range(4)], axis=1)
     hg_ref[...] = dot_nt(whole, win[...]).astype(BF16)
+    hg_copy = pltpu.make_async_copy(hg_ref, hg_hbm, local_sem.at[11])
+    hg_copy.start()
 
     o_copies[1].wait_recv()
     o_far.wait_recv()
     for k in range(LV):
         base = jnp.concatenate([streams[b, k, own_frames, :] for b in range(4)], axis=1).astype(F32)
-        out_ref[k] = (
+        out_ref[:, k, :] = (
             base + opart[k, own_frames, :].astype(F32) + o_core[1, k].astype(F32) + o_x[k].astype(F32)
         ).astype(BF16)
+    out_copy = pltpu.make_async_copy(out_ref, out_hbm, local_sem.at[12])
+    out_copy.start()
     for k in range(LV):
         final_step(k)
+    tg_copy = pltpu.make_async_copy(tg_ref, tg_hbm, local_sem.at[13])
+    tg_copy.start()
 
     for copy in started:
         copy.wait_send()
+    for copy in (hg_copy, out_copy, tg_copy):
+        copy.wait()
     assert len(started) <= COPIES
+
+
+def hand_over(out_in, hg_in, tg_in, out_ref, hg_ref, tg_ref, out_held, hg_held, tg_held, sem):
+    held = (out_held, hg_held, tg_held)
+    first = [
+        pltpu.make_async_copy(a, b, sem.at[i]) for i, (a, b) in enumerate(zip((out_in, hg_in, tg_in), held))
+    ]
+    second = [
+        pltpu.make_async_copy(a, b, sem.at[3 + i])
+        for i, (a, b) in enumerate(zip(held, (out_ref, hg_ref, tg_ref)))
+    ]
+    for copy in first:
+        copy.start()
+    for before, after in zip(first, second):
+        before.wait()
+        after.start()
+    for copy in second:
+        copy.wait()
 
 
 def shards(
     hidden, code_ids, lengths, weight_in, weight_query, weight_key, weight_value, weight_out,
     norm_gain, tables, upstream,
 ):
-    vmem = pl.BlockSpec(memory_space=pltpu.VMEM)
-    hbm = pl.BlockSpec(memory_space=pltpu.HBM)
+    hbm = pl.BlockSpec(memory_space=pl.ANY)
 
     def scratch(dtype, *shape):
         return pltpu.VMEM(shape, dtype)
 
     block = (LV, FR, COLS)
-    out, hidden_grad, table_grad = pl.pallas_call(
+    shapes = (
+        jax.ShapeDtypeStruct((OWN, LV, WIDTH), BF16),
+        jax.ShapeDtypeStruct((FR, WIDTH), BF16),
+        jax.ShapeDtypeStruct((ENT, LV, COLS), F32),
+    )
+    results = pl.pallas_call(
         kernel,
-        out_shape=(
-            jax.ShapeDtypeStruct((LV, OWN, WIDTH), BF16),
-            jax.ShapeDtypeStruct((FR, WIDTH), BF16),
-            jax.ShapeDtypeStruct((LV, ENT, COLS), F32),
-        ),
+        out_shape=shapes,
         in_specs=[hbm] * 11,
-        out_specs=(vmem, vmem, vmem),
+        out_specs=(hbm, hbm, hbm),
         scratch_shapes=[
+            scratch(BF16, OWN, LV, WIDTH),
+            scratch(BF16, FR, WIDTH),
+            scratch(F32, ENT, LV, COLS),
+            scratch(BF16, ENT, LV, COLS),
+            scratch(BF16, OWN, LV, WIDTH),
             scratch(jnp.int32, 8, FR),
             pltpu.SMEM((4,), jnp.int32),
             scratch(F32, 1, WIDTH),
@@ -692,20 +729,20 @@
             scratch(BF16, LV, 2, ENT, COLS),
             scratch(BF16, 4, LV, ENT, COLS),
             scratch(BF16, 4, LV, ENT, COLS),
-            pltpu.SemaphoreType.DMA((11,)),
+            pltpu.SemaphoreType.DMA((14,)),
             pltpu.SemaphoreType.DMA((COPIES,)),
             pltpu.SemaphoreType.DMA((COPIES,)),
         ],
         compiler_params=pltpu.CompilerParams(
-            collective_id=0, has_side_effects=True, vmem_limit_bytes=53 << 20
+            collective_id=0, has_side_effects=True, vmem_limit_bytes=VMEM_BYTES
         ),
         name="layer",
     )(
         code_ids.T,
         lengths,
         norm_gain.reshape(1, WIDTH),
-        jnp.transpose(tables, (1, 0, 2)),
-        jnp.transpose(upstream, (1, 0, 2)),
+        tables,
+        upstream,
         hidden,
         weight_in,
         weight_query,
@@ -713,11 +750,15 @@
         weight_value,
         weight_out,
     )
-    return (
-        jnp.transpose(out, (1, 0, 2)),
-        hidden_grad,
-        jnp.transpose(table_grad, (1, 0, 2)),
-    )
+    return pl.pallas_call(
+        hand_over,
+        out_shape=shapes,
+        in_specs=[hbm] * 3,
+        out_specs=(hbm, hbm, hbm),
+        scratch_shapes=[pltpu.VMEM(x.shape, x.dtype) for x in shapes] + [pltpu.SemaphoreType.DMA((6,))],
+        compiler_params=pltpu.CompilerParams(vmem_limit_bytes=VMEM_BYTES),
+        name="hand_over",
+    )(*results)
 
 
 def solution(mesh):

time: 88.1 us -> 83.7 us (0.950)
  local copies, waits for them, and re-layouts: 6.96 us -> 0 us
  Pallas kernels: 79.9 us -> 82.5 us
    unnamed x11 -> x0, local copies, waits for them, and re-layouts: 6.96 us -> none
    pallas_call x1 -> x2, Pallas kernels: 79.9 us -> 82.5 us  [the longest x1 80.7 us: shards(): pl.pallas_call(kernel, out_shape=shapes, in_specs=[hbm] * 11, out_specs=(...]
where the time goes in v3:
time: 83.7 us; the launch traced here: 83.2 us
  Pallas kernels  82.5 us (99%)
    pallas_call x1, Pallas kernels, shards(): pl.pallas_call(kernel, out_shape=shapes, in_specs=[hbm] * 11, out_specs=(...  80.7 us
    pallas_call x1, Pallas kernels, shards(): pl.pallas_call(hand_over, out_shape=shapes, in_specs=[hbm] * 3, out_specs...  1.83 us

profile of v3, /device:TPU:4, one launch (start us, length us, event | category | flops | bytes accessed | tf_op | source)
XLA Modules:
  0.0 83.2 jit_solution(8122834426206238393)
XLA Ops:
  0.6 80.7 %layer.1 = (bf16[32,4,1024]{2,1,0:T(4,128)(2,1)}, bf16[128,1024]{1,0:T(8,128)(2,1)}, f32[32,4,256]{2,1,0:T(4,128)}) custom-call(s32[4,128]{1,0:T(4,128)} %bitcast.3, s32[4]{0:T(128)} %lens_hbm.1, f32[1,1024]{1,0:T(1,128)} %bitcast.2, bf16[32,4,256]{2,1,0:T(4,128)(2,1)} %tab_hbm.1, bf16[32,4,1024]{2,1,0:T(4,128)(2,1)} %up_hbm.1, bf16[128,1024]{1,0:T(8,128)(2,1)} %hid_hbm.1, ...), custom_call_target="tpu_custom_call" | custom-call | tf_op jit(solution)/shard_map/layer/pallas_call | solution.py:658
  81.3 1.8 %hand_over.1 = (bf16[32,4,1024]{2,1,0:T(4,128)(2,1)}, bf16[128,1024]{1,0:T(8,128)(2,1)}, f32[32,4,256]{2,1,0:T(4,128)}) custom-call(bf16[32,4,1024]{2,1,0:T(4,128)(2,1)} %get-tuple-element.6.out_in, bf16[128,1024]{1,0:T(8,128)(2,1)} %get-tuple-element.7.hg_in, f32[32,4,256]{2,1,0:T(4,128)} %get-tuple-element.8.tg_in), custom_call_target="tpu_custom_call" | custom-call | tf_op jit(solution)/shard_map/hand_over/pallas_call | solution.py:753

commit v4 on v3

--- a/solution.py
+++ b/solution.py
@@ -38,7 +38,7 @@
     out_hbm, hg_hbm, tg_hbm,
     out_ref, hg_ref, tg_ref,
     tab_in, up_in, codes_ref, lens_ref, gain_ref, hid_ref, win, wq, wk, wv, wo,
-    nbr, prev, tab, oh, oht, ups, ctx_send, ctx_core, ctx_mid, ctx_x,
+    nbr, raw, prev, tab, oh, oht, ups, ctx_send, ctx_core, ctx_mid, ctx_x,
     look, relay, fin, stream_own, streams, normed, scale,
     qs, ks, vs, gms, prod, sums, mix, gqs, gks, gvs, gk_sum, gv_sum,
     pn, pn_own, pn_core, pn_mid, pn_x, stat_wide, stat, stat_col,
@@ -62,8 +62,9 @@
         cc = 1 - core if dc else core
         return (yy * 16 + xx * 8 + zz, hh * 2 + cc)
 
-    seq_next = (lax.rem(seq + 1, 64), lvl)
-    seq_back = (lax.rem(seq + 63, 64), lvl)
+    shifts = (0, 16, 48, 32)
+    seq_next = [(lax.rem(seq + 1 + shift, 64), lvl) for shift in shifts]
+    seq_back = [(lax.rem(seq + 127 - shift, 64), lvl) for shift in shifts]
     y_up, y_down, y_far = device(dy=1), device(dy=-1), device(dy=2)
     z_up, z_down, z_up2, z_down2 = device(dz=1), device(dz=-1), device(dz=2), device(dz=-2)
     x_near, x_far, mate, cross = device(dx=1), device(dh=1), device(dc=1), device(dh=1, dc=1)
@@ -119,7 +120,7 @@
         fetch[name].start()
 
     barrier = pltpu.get_barrier_semaphore()
-    for source in (z_up, z_down, z_up2, z_down2, x_near, y_up, y_down, y_far, mate, x_far, cross, seq_back):
+    for source in (z_up, z_down, z_up2, z_down2, x_near, y_up, y_down, y_far, mate, x_far, cross, *seq_back):
         pl.semaphore_signal(barrier, inc=1, device_id=source, device_id_type=MESH)
     fetch["hid"].wait()
     fetch["win"].wait()
@@ -130,7 +131,7 @@
     for k in range(LV):
         tab[k, own_rows, :] = tab_in[:, k, :]
     fetch["codes"].wait()
-    pl.semaphore_wait(barrier, 12)
+    pl.semaphore_wait(barrier, 15)
 
     def block(half, xx, zz):
         return tab.at[2 * half : 2 * half + 2, block_rows(xx, zz)]
@@ -143,7 +144,12 @@
         near_own.append(push(own[h], x_near))
         up1.append(push(own[h], z_up))
         down1.append(push(own[h], z_down))
-    code_copy = send(codes_ref, nbr, seq_next)
+    code_copies = [send(codes_ref, nbr.at[i], target) for i, target in enumerate(seq_next)]
+    code_copies += [
+        send(codes_ref, raw.at[1], y_up),
+        send(codes_ref, raw.at[2], y_down),
+        send(codes_ref, raw.at[3], y_far),
+    ]
     ctx_copies = [
         send(ctx_send.at[lvl_cross], ctx_core.at[0], mate),
         send(ctx_send.at[lvl_mate], ctx_core.at[1], mate),
@@ -170,28 +176,25 @@
         near1.append(push(block(h, xl, z - 1), x_near))
         down1[h].wait_recv()
         near1.append(push(block(h, xl, z + 1), x_near))
-
-    code_copy.wait_recv()
-    lane8 = lax.broadcasted_iota(jnp.int32, (8, FR), 1)
-    sub8 = lax.broadcasted_iota(jnp.int32, (8, FR), 0)
-    own_codes = codes_ref[...]
-    shifted = pltpu.roll(own_codes, 1, 1)
-    incoming = pltpu.roll(nbr[...], 1, 1)
-    incoming = jnp.where(jnp.broadcast_to(seq, (8, FR)) == 0, 0, incoming)
-    shifted = jnp.where(lane8 == 0, incoming, shifted)
-    first_row = jnp.broadcast_to(shifted[LV - 1 : LV, :], (8, FR))
-    prev[0] = jnp.where(sub8 == 0, first_row, pltpu.roll(own_codes, 1, 0))
-    code_y = [
-        send(prev.at[0], prev.at[1], y_up),
-        send(prev.at[0], prev.at[2], y_down),
-        send(prev.at[0], prev.at[3], y_far),
-    ]
     ctx_copies[0].wait_recv()
     ctx_mid[...] = (ctx_send[lvl_far].astype(F32) + ctx_core[0].astype(F32)).astype(BF16)
     ctx_far = send(ctx_mid, ctx_x, x_far)
 
-    for copy in code_y:
+    for copy in code_copies:
         copy.wait_recv()
+    raw[0] = codes_ref[...]
+    lane8 = lax.broadcasted_iota(jnp.int32, (8, FR), 1)
+    sub8 = lax.broadcasted_iota(jnp.int32, (8, FR), 0)
+    for slot, shift in enumerate(shifts):
+        codes = raw[slot]
+        shifted = pltpu.roll(codes, 1, 1)
+        incoming = pltpu.roll(nbr[slot], 1, 1)
+        holder = lax.rem(seq + 64 - shift, 64)
+        incoming = jnp.where(jnp.broadcast_to(holder, (8, FR)) == 0, 0, incoming)
+        shifted = jnp.where(lane8 == 0, incoming, shifted)
+        first_row = jnp.broadcast_to(shifted[LV - 1 : LV, :], (8, FR))
+        prev[slot] = jnp.where(sub8 == 0, first_row, pltpu.roll(codes, 1, 0))
+
     first = y * RANGE
     by_lane = lax.broadcasted_iota(jnp.int32, (FR, RANGE), 1) + first
     by_row = lax.broadcasted_iota(jnp.int32, (RANGE, FR), 0) + first
@@ -228,9 +231,6 @@
     for i in range(4):
         retain = jnp.where(frame == begin, 0.0, retain)
         begin = begin + lens_ref[i]
-    ctx_copies[1].wait_recv()
-    ctx_far.wait_recv()
-    context = ctx_send[lvl].astype(F32) + ctx_core[1].astype(F32) + ctx_x[...].astype(F32)
 
     top, low = slice(0, FR // 2), slice(FR // 2, FR)
     relay_up, relay_down = [], []
@@ -296,6 +296,9 @@
     relayed(2)
     direct(3)
     relayed(3)
+    ctx_copies[1].wait_recv()
+    ctx_far.wait_recv()
+    context = ctx_send[lvl].astype(F32) + ctx_core[1].astype(F32) + ctx_x[...].astype(F32)
     stream(0)
     stream(1)
     stream(2)
@@ -412,6 +415,17 @@
     norm(3)
     two_levels(2)
 
+    gq = gqs[...].reshape(LV * FR, COLS)
+    gk = gks[...].reshape(LV * FR, COLS)
+    gv = gvs[...].reshape(LV * FR, COLS)
+
+    def partial(owner):
+        w = rows(owner * COLS, COLS)
+        total = dot_nt(gq, wq[w, :]) + dot_nt(gk, wk[w, :]) + dot_nt(gv, wv[w, :])
+        return total.reshape(LV, FR, COLS)
+
+    pn[0] = partial(lvl_cross).astype(BF16)
+    pn_cross = [send(pn.at[0, k], pn_core.at[0, k], mate) for k in range(LV)]
     def stat_body(i, carry):
         r = rows(i * 32, 32)
         for k in range(LV):
@@ -434,17 +448,6 @@
         send(stat.at[0], stat.at[3], cross),
     ]
 
-    gq = gqs[...].reshape(LV * FR, COLS)
-    gk = gks[...].reshape(LV * FR, COLS)
-    gv = gvs[...].reshape(LV * FR, COLS)
-
-    def partial(owner):
-        w = rows(owner * COLS, COLS)
-        total = dot_nt(gq, wq[w, :]) + dot_nt(gk, wk[w, :]) + dot_nt(gv, wv[w, :])
-        return total.reshape(LV, FR, COLS)
-
-    pn[0] = partial(lvl_cross).astype(BF16)
-    pn_cross = [send(pn.at[0, k], pn_core.at[0, k], mate) for k in range(LV)]
     pn[2] = partial(lvl_far).astype(BF16)
     pn_far = []
     for k in range(LV):
@@ -515,7 +518,7 @@
     pass_grad(2)
 
     half = ENT // 2
-    fringe, crossed, direct_sums = [], [], []
+    fringe, crossed, direct_sums = {}, {}, {}
 
     def packed(xx, zz, k):
         return grads[k, block_rows(xx, zz), :]
@@ -530,7 +533,7 @@
             value = packed(xx, z + 4, k).astype(BF16)
             f4_send[0, k, j] = value[0:half, :]
             f4_send[1, k, j] = value[half:, :]
-        fringe.append(
+        fringe[k] = (
             [
                 send(f3_send.at[0, k], f3_recv.at[0, k], z_down),
                 send(f3_send.at[1, k], f3_recv.at[1, k], z_up),
@@ -540,7 +543,7 @@
         )
         for o in range(3):
             c1_send[k, o] = packed(1 - xl, z + o - 1, k).astype(BF16)
-        crossed.append([send(c1_send.at[k], c1_recv.at[k], x_near)])
+        crossed[k] = [send(c1_send.at[k], c1_recv.at[k], x_near)]
 
     def two_away(side, j, k):
         value = packed(xl if j == 0 else 1 - xl, z - 2 if side == 0 else z + 2, k)
@@ -564,7 +567,7 @@
             d_send[2 + side, k] = value.astype(BF16)
             value = packed(xl, z + 2 * side - 1, k) + c1_recv[k, 2 * side].astype(F32)
             d_send[side, k] = value.astype(BF16)
-        direct_sums.append(
+        direct_sums[k] = (
             [
                 send(d_send.at[i, k], d_recv.at[i, k], target)
                 for i, target in ((2, z_down2), (3, z_up2), (0, z_down), (1, z_up))
@@ -581,18 +584,18 @@
 
     fringe_step(0)
     fringe_step(1)
+    fringe_step(3)
     fringe_step(2)
-    fringe_step(3)
     cross_step(0)
     cross_step(1)
     direct_step(0)
+    cross_step(3)
     cross_step(2)
-    cross_step(3)
     cg_far.wait_recv()
     cg_pass = push(cgs.at[lvl_far], mate)
     direct_step(1)
+    direct_step(3)
     direct_step(2)
-    direct_step(3)
 
     cg_mate.wait_recv()
     cg_pass.wait_recv()
@@ -675,7 +678,8 @@
             scratch(BF16, WIDTH, COLS),
             scratch(BF16, WIDTH, COLS),
             scratch(BF16, COLS, WIDTH),
-            scratch(jnp.int32, 8, FR),
+            scratch(jnp.int32, NY, 8, FR),
+            scratch(jnp.int32, NY, 8, FR),
             scratch(jnp.int32, NY, 8, FR),
             scratch(BF16, LV, RANGE, COLS),
             scratch(BF16, LV, NY * FR, RANGE),

time: 83.7 us -> 81.2 us (0.970)
  Pallas kernels: 82.5 us -> 80.5 us
    pallas_call x1, Pallas kernels: 80.7 us -> 78.6 us  [shards(): pl.pallas_call(kernel, out_shape=shapes, in_specs=[hbm] * 11, out_specs=(...]
where the time goes in v4:
time: 81.2 us; the launch traced here: 81.1 us
  Pallas kernels  80.5 us (99%)
    pallas_call x1, Pallas kernels, shards(): pl.pallas_call(kernel, out_shape=shapes, in_specs=[hbm] * 11, out_specs=(...  78.6 us
    pallas_call x1, Pallas kernels, shards(): pl.pallas_call(hand_over, out_shape=shapes, in_specs=[hbm] * 3, out_specs...  1.83 us

profile of v4, /device:TPU:4, one launch (start us, length us, event | category | flops | bytes accessed | tf_op | source)
XLA Modules:
  0.0 81.1 jit_solution(7708860814590009911)
XLA Ops:
  0.6 78.6 %layer.1 = (bf16[32,4,1024]{2,1,0:T(4,128)(2,1)}, bf16[128,1024]{1,0:T(8,128)(2,1)}, f32[32,4,256]{2,1,0:T(4,128)}) custom-call(s32[4,128]{1,0:T(4,128)} %bitcast.3, s32[4]{0:T(128)} %lens_hbm.1, f32[1,1024]{1,0:T(1,128)} %bitcast.2, bf16[32,4,256]{2,1,0:T(4,128)(2,1)} %tab_hbm.1, bf16[32,4,1024]{2,1,0:T(4,128)(2,1)} %up_hbm.1, bf16[128,1024]{1,0:T(8,128)(2,1)} %hid_hbm.1, ...), custom_call_target="tpu_custom_call" | custom-call | tf_op jit(solution)/shard_map/layer/pallas_call | solution.py:661
  79.3 1.8 %hand_over.1 = (bf16[32,4,1024]{2,1,0:T(4,128)(2,1)}, bf16[128,1024]{1,0:T(8,128)(2,1)}, f32[32,4,256]{2,1,0:T(4,128)}) custom-call(bf16[32,4,1024]{2,1,0:T(4,128)(2,1)} %get-tuple-element.6.out_in, bf16[128,1024]{1,0:T(8,128)(2,1)} %get-tuple-element.7.hg_in, f32[32,4,256]{2,1,0:T(4,128)} %get-tuple-element.8.tg_in), custom_call_target="tpu_custom_call" | custom-call | tf_op jit(solution)/shard_map/hand_over/pallas_call | solution.py:757
